TPU v7x, 32 devices: a whole 2x2x4 slice. The times are simulated.
32 devices in a mesh: dp: 16 (over z, y, x), tensor: 2 (over core).
Axes of the slice: x: 2, y: 2, z: 4, core: 2. Of those that a mesh axis runs over, the one named last changes fastest.
Arguments:
- tokens: bfloat16 [16, 1024, 1024], P('dp'), may hold values from -6 to 6
- cotangent: bfloat16 [16, 1024, 1024], P('dp'), may hold values from -6 to 6
- lengths: int32 [16], P('dp'), may hold values from 128 to 1024, as said below
- noise_times: int32 [16], P('dp'), may hold values from 0 to 255
- query_weight: bfloat16 [1024, 1024], P(None, 'tensor'), may hold values from -0.1875 to 0.1875
- key_weight: bfloat16 [1024, 1024], P(None, 'tensor'), may hold values from -0.1875 to 0.1875
- value_weight: bfloat16 [1024, 1024], P(None, 'tensor'), may hold values from -0.1875 to 0.1875
- merge_weight: bfloat16 [1024, 1024], P('tensor'), may hold values from -0.75 to 0.75
- up_weight: bfloat16 [1024, 4096], P(None, 'tensor'), may hold values from -0.1875 to 0.1875
- down_weight: bfloat16 [4096, 1024], P('tensor'), may hold values from -0.09375 to 0.09375
- first_scales: float32 [256, 1024], replicated, may hold values from 0.1 to 1.9
- second_scales: float32 [256, 1024], replicated, may hold values from 0.1 to 1.9
Outputs:
- layer_output: bfloat16 [16, 1024, 1024], P('dp')
- grad_tokens: bfloat16 [16, 1024, 1024], P('dp')
- grad_query: float32 [1024, 1024], P('dp', 'tensor')
- grad_key: float32 [1024, 1024], P('dp', 'tensor')
- grad_value: float32 [1024, 1024], P('dp', 'tensor')
- grad_merge: float32 [1024, 1024], P('tensor', 'dp')
- grad_up: float32 [1024, 4096], P('dp', 'tensor')
- grad_down: float32 [4096, 1024], P('tensor', 'dp')
- grad_first: float32 [256, 1024], P(None, 'dp')
- grad_second: float32 [256, 1024], P(None, 'dp')
Inputs may be any that keep to these rules, and one draw needn't show every extreme that they name: `lengths`: some sequence has exactly 1024 tokens; the others have at least 128.
All inputs are finite; a program needn't handle non-finite values.
Results may differ from a plain program's by a relative error of at most 0.014.
Values sent between devices are 32-bit elements; how exact they have to be, the bound alone decides.
A program may use at most 192 MiB of HBM per device.

v0:
```python
import functools
import math

import jax
import jax.numpy as jnp
import numpy as np
from jax import lax
from jax.experimental import pallas as pl
from jax.experimental.pallas import tpu as pltpu
from jax.sharding import PartitionSpec as P

HEAD = 64
MESH = pl.DeviceIdType.MESH


epsilon = 1e-05
highest = lax.Precision.HIGHEST


def gelu_tanh(values):
    return (
        0.5
        * values
        * (1.0 + jnp.tanh(0.7978845608028654 * (values + 0.044715 * values * values * values)))
    )


def rope_tables(length, head_size):
    halves = head_size // 2
    places = jnp.arange(length, dtype=jnp.float32)[:, None]
    frequency = jnp.exp(
        jnp.arange(halves, dtype=jnp.float32) * (-2.0 * math.log(10000.0) / head_size)
    )
    angles = places * frequency[None, :]
    return (jnp.cos(angles), jnp.sin(angles))


def rotate(values, cos_table, sin_table):
    halves = values.shape[-1] // 2
    first_half = values[..., :halves]
    second_half = values[..., halves:]
    cosine = cos_table[:, None, :]
    sine_part = sin_table[:, None, :]
    return jnp.concatenate(
        [
            first_half * cosine - second_half * sine_part,
            second_half * cosine + first_half * sine_part,
        ],
        axis=-1,
    )


def unrotate(gradient, cos_table, sin_table):
    halves = gradient.shape[-1] // 2
    first_half = gradient[..., :halves]
    second_half = gradient[..., halves:]
    cosine = cos_table[:, None, :]
    sine_part = sin_table[:, None, :]
    return jnp.concatenate(
        [
            first_half * cosine + second_half * sine_part,
            second_half * cosine - first_half * sine_part,
        ],
        axis=-1,
    )


def normalize(values):
    centred = values - jnp.mean(values, axis=-1, keepdims=True)
    inv_std = lax.rsqrt(jnp.mean(centred * centred, axis=-1, keepdims=True) + epsilon)
    return (centred * inv_std, inv_std)


def norm_back(grad_norm, normed, inv_std, scale_rows):
    grad_hat = grad_norm * scale_rows[:, None, :]
    grad_scale = jnp.sum(grad_norm * normed, axis=1)
    mean_grad = jnp.mean(grad_hat, axis=-1, keepdims=True)
    mean_cross = jnp.mean(grad_hat * normed, axis=-1, keepdims=True)
    return (inv_std * (grad_hat - mean_grad - normed * mean_cross), grad_scale)


def block_scores(query_block, key_rot, key_bias, scale_factor):
    scores = jnp.einsum("sqhd,skhd->shqk", query_block, key_rot, preferred_element_type=jnp.float32)
    return scores * scale_factor + key_bias[:, None, None, :]


def rope_lanes(length):
    halves = HEAD // 2
    places = np.arange(length, dtype=np.float64)[:, None]
    frequency = np.exp(np.arange(halves) * (-2.0 * math.log(10000.0) / HEAD))
    angles = places * frequency[None, :]
    cosine, sine = np.cos(angles), np.sin(angles)
    return (
        np.concatenate([cosine] * 4, axis=1).astype(np.float32),
        np.concatenate([-sine, sine] * 2, axis=1).astype(np.float32),
    )


def swap_halves(values):
    lanes = lax.broadcasted_iota(jnp.int32, values.shape, 1)
    first = lax.rem(lanes, HEAD) < HEAD // 2
    half = HEAD // 2
    return jnp.where(first, pltpu.roll(values, 128 - half, 1), pltpu.roll(values, half, 1))


def centre(values):
    middle = jnp.mean(values, axis=1, keepdims=True)
    centred = values - middle
    inverse = lax.rsqrt(jnp.mean(centred * centred, axis=1, keepdims=True) + epsilon)
    return centred * inverse


NT = (((1,), (1,)), ((), ()))


def mm(a, b):
    return jnp.dot(a, b, preferred_element_type=jnp.float32)


def mm_nt(a, b):
    return lax.dot_general(a, b, NT, preferred_element_type=jnp.float32)


def forward_kernel(
    names, length_ref, tokens, cotangent, scale_one, scale_two, cosine, sine, wq, wk, wv, wm, wu,
    q_out, k_out, v_out, heads, heads_t, lse, hidden, act, slope, mlp_t,
    nin, vq, vk, vv, vm, vu, other_m, v_t, send_m, recv_m, send_o, recv_o, bias, wsem, ssem, rsem,
):
    rows, width = tokens.shape
    pairs = q_out.shape[0]
    here = {n: lax.axis_index(n) for n in names}
    other = {**here, names[1]: 1 - here[names[1]]}
    other = tuple(other[n] for n in names)
    loads = [
        pltpu.make_async_copy(a, b, wsem.at[i])
        for i, (a, b) in enumerate(((wq, vq), (wk, vk), (wv, vv), (wm, vm), (wu, vu)))
    ]
    for c in loads:
        c.start()
    barrier = pltpu.get_barrier_semaphore()
    pl.semaphore_signal(barrier, inc=1, device_id=other, device_id_type=MESH)
    pl.semaphore_wait(barrier, 1)
    length = length_ref[0]

    def place(start, count):
        return start + lax.broadcasted_iota(jnp.int32, (count, 1), 0)

    def mask_of(start, count):
        return jnp.where(place(start, count) < length, 1.0, 0.0)

    bias[...] = jnp.broadcast_to((mask_of(0, rows) - 1.0) * 1000000000.0, (rows, 128))

    def norm_rows(i, _):
        at = pl.multiple_of(i * 128, 128)
        x = tokens[pl.ds(at, 128), :].astype(jnp.float32) * mask_of(at, 128)
        nin[pl.ds(at, 128), :] = (centre(x) * scale_one[...]).astype(jnp.bfloat16)
        return 0

    lax.fori_loop(0, rows // 128, norm_rows, 0)
    for c in loads[:4]:
        c.wait()
    send_m[...] = vm[...].astype(jnp.float32)
    merge_copy = pltpu.make_async_remote_copy(
        src_ref=send_m, dst_ref=recv_m, send_sem=ssem.at[0], recv_sem=rsem.at[0],
        device_id=other, device_id_type=MESH,
    )
    merge_copy.start()

    def project(i, _):
        at = pl.multiple_of(i * 256, 256)
        own = pl.ds(at, 256)
        x = nin[own, :]
        c, s = cosine[own, :], sine[own, :]
        for ref, w in ((q_out, vq), (k_out, vk)):
            y = mm(x, w[...])
            for p in range(pairs):
                part = y[:, 128 * p : 128 * p + 128]
                ref[p, own, :] = (part * c + swap_halves(part) * s).astype(jnp.bfloat16)
        y = mm(x, vv[...])
        for p in range(pairs):
            part = y[:, 128 * p : 128 * p + 128]
            v_out[p, own, :] = part.astype(jnp.bfloat16)
            v_t[p, :, own] = part.T.astype(jnp.bfloat16)
        return 0

    lax.fori_loop(0, rows // 256, project, 0)

    def o_copy(p):
        return pltpu.make_async_remote_copy(
            src_ref=send_o.at[p], dst_ref=recv_o.at[p], send_sem=ssem.at[1 + p], recv_sem=rsem.at[1 + p],
            device_id=other, device_id_type=MESH,
        )

    lane = lax.broadcasted_iota(jnp.int32, (rows, 128), 1)
    block = 512

    def attend(p, _):
        for h in range(2):
            keys = jnp.where((lane < HEAD) == (h == 0), k_out[p] * 0.125, 0.0).astype(jnp.bfloat16)
            values_t = v_t[p, pl.ds(HEAD * h, HEAD), :]
            for b in range(rows // block):
                cols = pl.ds(b * block, block)
                s = mm_nt(keys, q_out[p, cols, :]) + bias[:, :1]
                peak = jnp.max(s, axis=0, keepdims=True)
                e = jnp.exp(s - peak)
                total = jnp.sum(e, axis=0, keepdims=True)
                o = mm(values_t, e.astype(jnp.bfloat16)) / total
                heads_t[p, pl.ds(HEAD * h, HEAD), cols] = o.astype(jnp.bfloat16)
                lse[pl.ds(2 * p + h, 1), cols] = peak + jnp.log(total)
        o = heads_t[p].astype(jnp.float32).T
        send_o[p] = o
        heads[p] = o.astype(jnp.bfloat16)
        o_copy(p).start()
        count = rows // pairs
        at = pl.multiple_of(p * count, count)
        turned = (cotangent[pl.ds(at, count), :].astype(jnp.float32) * mask_of(at, count)).T
        mlp_t[:, :, pl.ds(at, count)] = turned.astype(jnp.bfloat16).reshape(mlp_t.shape[0], mlp_t.shape[1], count)
        return 0

    lax.fori_loop(0, pairs, attend, 0)
    merge_copy.wait()
    other_m[...] = recv_m[...].astype(jnp.bfloat16)
    for p in range(pairs):
        o_copy(p).wait()
    loads[4].wait()

    def finish(i, _):
        at = pl.multiple_of(i * 256, 256)
        own = pl.ds(at, 256)
        mine = jnp.concatenate([heads[p, own, :] for p in range(pairs)], axis=1)
        theirs = jnp.concatenate([recv_o[p, own, :].astype(jnp.bfloat16) for p in range(pairs)], axis=1)
        attn = mm(mine, vm[...]) + mm(theirs, other_m[...])
        one = tokens[own, :].astype(jnp.float32) * mask_of(at, 256) + attn
        hidden[own, :] = one
        normal = (centre(one) * scale_two[...]).astype(jnp.bfloat16)
        for j in range(0, vu.shape[1], 512):
            v = mm(normal, vu[:, j : j + 512])
            square = v * v
            t = jnp.tanh(0.7978845608028654 * v * (1.0 + 0.044715 * square))
            up = 0.5 * (1.0 + t)
            act[own, j : j + 512] = (v * up).astype(jnp.bfloat16)
            slope[own, j : j + 512] = (
                up + 0.5 * v * (1.0 - t * t) * (0.7978845608028654 * (1.0 + 0.134145 * square))
            ).astype(jnp.bfloat16)
        return 0

    lax.fori_loop(0, rows // 256, finish, 0)


def forward(names, length, tokens, cotangent, scale_one, scale_two, cosine, sine, wq, wk, wv, wm, wu):
    rows, width = tokens.shape
    local, units = wq.shape[1], wu.shape[1]
    pairs = local // 128
    vmem = pl.BlockSpec(memory_space=pltpu.VMEM)
    hbm = pl.BlockSpec(memory_space=pl.ANY)
    half = jnp.bfloat16
    full = jnp.float32
    shapes = [
        ((pairs, rows, 128), half),
        ((pairs, rows, 128), half),
        ((pairs, rows, 128), half),
        ((pairs, rows, 128), half),
        ((pairs, 128, rows), half),
        ((2 * pairs, rows), full),
        ((rows, width), full),
        ((rows, units), half),
        ((rows, units), half),
        ((16, width // 16, rows), half),
    ]
    return pl.pallas_call(
        functools.partial(forward_kernel, names),
        out_shape=[jax.ShapeDtypeStruct(*s) for s in shapes],
        in_specs=[pl.BlockSpec(memory_space=pltpu.SMEM)] + [vmem] * 6 + [hbm] * 5,
        out_specs=[vmem] * len(shapes),
        scratch_shapes=[
            pltpu.VMEM((rows, width), half),
            pltpu.VMEM(wq.shape, half),
            pltpu.VMEM(wk.shape, half),
            pltpu.VMEM(wv.shape, half),
            pltpu.VMEM(wm.shape, half),
            pltpu.VMEM(wu.shape, half),
            pltpu.VMEM(wm.shape, half),
            pltpu.VMEM((pairs, 128, rows), half),
            pltpu.VMEM(wm.shape, full),
            pltpu.VMEM(wm.shape, full),
            pltpu.VMEM((pairs, rows, 128), full),
            pltpu.VMEM((pairs, rows, 128), full),
            pltpu.VMEM((rows, 128), full),
            pltpu.SemaphoreType.DMA((5,)),
            pltpu.SemaphoreType.DMA((1 + pairs,)),
            pltpu.SemaphoreType.DMA((1 + pairs,)),
        ],
        compiler_params=pltpu.CompilerParams(collective_id=1, has_side_effects=True, vmem_limit_bytes=58 * 2**20),
        name="forward",
    )(length, tokens, cotangent, scale_one, scale_two, cosine, sine, wq, wk, wv, wm, wu)


ITEMS = 24
TILE = 256
RING = 5
HELD = 12
LAGS = (4, 7, 9, 11)
FIRSTS = (0, 8, 16, 18, 24)


def count_from(i, starts):
    total = 0
    for start in starts:
        total = total + jnp.where(i >= start, 1, 0)
    return total


def flip(index, weight):
    return index + weight * (1 - 2 * lax.rem(lax.div(index, weight), 2))


def weight_of(color, stage):
    k = lax.rem(color + stage, 3)
    return 1 + (k * (k + 1)) // 2


def color_of(i):
    return lax.rem(lax.rem(i, 8), 3)


def slot_of(i):
    return count_from(i, (8, 16)) - 2 * count_from(i, (18,))


def backward_kernel(
    names, length_ref, moment, scale_one, scale_two,
    l_down, r_down, heads, q_in, k_in, v_in, heads_t, lse_in, cosine, sine,
    merge_in, wq, wk, wv, tokens, hidden, slope, cotangent, wu, wd,
    out, rows_out, tokens_out, layer_out, r_up, hidden_grad,
    left, s1, r1, r2, r3, r4, rb, qkv, send_p, recv_p, ga, terms,
    lsem, fsem, ssem, csem, psem, qsem, gsem, jsem, credit, credit_two, core_free,
):
    here = {n: lax.axis_index(n) for n in names}
    d = here[names[0]]

    def device(**moved):
        at = {**here, **moved}
        return tuple(at[n] for n in names)

    core = device(**{names[1]: 1 - here[names[1]]})

    def across(weight):
        return device(**{names[0]: flip(d, weight)})

    def absolute(r):
        total = 0
        for b in range(4):
            bit = lax.rem(lax.div(d, 2**b), 2)
            total = total + (2**b) * (1 - bit if (r >> b) & 1 else bit)
        return total

    def load_left(source, slot):
        for r in range(16):
            pltpu.make_async_copy(source.at[absolute(r)], left.at[slot, r], lsem).start()

    def left_loaded(slot):
        pltpu.make_async_copy(left.at[slot], left.at[slot], lsem).wait()

    def turn(values, slot, own):
        turned = values.T.astype(jnp.bfloat16)
        for c in range(16):
            left[slot, absolute(c), :, own] = turned[64 * c : 64 * c + 64]

    load_left(l_down, 0)
    barrier = pltpu.get_barrier_semaphore()
    for weight in (1, 2, 4, 8):
        pl.semaphore_signal(barrier, inc=1, device_id=across(weight), device_id_type=MESH)
    pl.semaphore_signal(barrier, inc=1, device_id=core, device_id_type=MESH)
    pl.semaphore_wait(barrier, 5)

    def fetch(i, lane):
        slot = lax.rem(i, 2)
        target, sem = rb.at[lane, slot], fsem.at[lane, slot]
        for g, source in ((0, r_down), (1, r_up)):
            @pl.when((i >= FIRSTS[g]) & (i < FIRSTS[g + 1]))
            def _():
                col = pl.multiple_of((i - FIRSTS[g]) * TILE, TILE)
                pltpu.make_async_copy(source.at[:, pl.ds(col, TILE)], target, sem).start()

        @pl.when((i >= FIRSTS[2]) & (i < FIRSTS[3]))
        def _():
            for k in range(2):
                pltpu.make_async_copy(
                    heads.at[2 * (i - FIRSTS[2]) + k], target.at[:, pl.ds(128 * k, 128)], sem
                ).start()

        @pl.when(i >= FIRSTS[3])
        def _():
            pltpu.make_async_copy(qkv.at[i - FIRSTS[3]], target, sem).start()

    def fetched(i, lane):
        slot = lax.rem(i, 2)
        pltpu.make_async_copy(rb.at[lane, slot], rb.at[lane, slot], fsem.at[lane, slot]).wait()

    def product(i, first, lane):
        color, slot = color_of(i), slot_of(i)
        weights = [weight_of(color, s) for s in range(3)] + [8]
        rows = []
        for bits in range(8):
            r = first * weights[0] + sum(((bits >> (2 - k)) & 1) * weights[1 + k] for k in range(3))
            rows.append(left[slot, r])
        lhs = jnp.concatenate(rows, axis=0)
        return mm(lhs, rb[lane, lax.rem(i, 2)]).reshape(8, 64, TILE)

    def copy(i, s):
        weight = weight_of(color_of(i), s) if s < 3 else 8
        src = (s1.at[lax.rem(i, RING)], r1.at[lax.rem(i, HELD), pl.ds(4, 4)], r2.at[lax.rem(i, HELD), pl.ds(2, 2)], r3.at[i, pl.ds(1, 1)])[s]
        dst = (r1.at[lax.rem(i, HELD)], r2.at[lax.rem(i, HELD)], r3.at[i], r4.at[i])[s]
        return pltpu.make_async_remote_copy(
            src_ref=src, dst_ref=dst, send_sem=ssem.at[s, i], recv_sem=csem.at[s, i],
            device_id=across(weight), device_id_type=MESH,
        )

    def tick(i):
        @pl.when(i < ITEMS)
        def _():
            @pl.when(i >= RING)
            def _():
                copy(i - RING, 0).wait_send()

            fetched(i, 0)
            s1[lax.rem(i, RING)] = product(i, 1, 0)

            @pl.when(i >= HELD)
            def _():
                pl.semaphore_wait(credit.at[color_of(i)], 1)

            copy(i, 0).start()

            @pl.when((i + 2 < ITEMS))
            def _():
                fetch(i + 2, 0)

        a = i - LAGS[0]

        @pl.when((a >= 0) & (a < ITEMS))
        def _():
            fetched(a, 1)
            copy(a, 0).wait_recv()
            r1[lax.rem(a, HELD)] += product(a, 0, 1)

            @pl.when(a >= HELD)
            def _():
                pl.semaphore_wait(credit_two.at[color_of(a)], 1)

            copy(a, 1).start()

            @pl.when(a + 2 < ITEMS)
            def _():
                fetch(a + 2, 1)

        b = i - LAGS[1]

        @pl.when((b >= 0) & (b < ITEMS))
        def _():
            copy(b, 1).wait_recv()
            r2[lax.rem(b, HELD)] += r1[lax.rem(b, HELD), 0:4]
            copy(b, 2).start()
            copy(b, 1).wait_send()

            @pl.when(b + HELD < ITEMS)
            def _():
                color = color_of(b + HELD)
                pl.semaphore_signal(
                    credit.at[color], inc=1, device_id=across(weight_of(color, 0)), device_id_type=MESH
                )

        c = i - LAGS[2]

        @pl.when((c >= 0) & (c < ITEMS))
        def _():
            copy(c, 2).wait_recv()
            r3[c] += r2[lax.rem(c, HELD), 0:2]
            copy(c, 3).start()
            copy(c, 2).wait_send()

            @pl.when(c + HELD < ITEMS)
            def _():
                color = color_of(c + HELD)
                pl.semaphore_signal(
                    credit_two.at[color], inc=1, device_id=across(weight_of(color, 1)), device_id_type=MESH
                )

        e = i - LAGS[3]

        @pl.when((e >= 0) & (e < ITEMS))
        def _():
            copy(e, 3).wait_recv()
            out[e] = r4[e, 0] + r3[e, 0]

    for lane in range(2):
        fetch(jnp.int32(0), lane)
        fetch(jnp.int32(1), lane)
    rows, width = tokens.shape
    pairs = q_in.shape[0]
    length = length_ref[0]
    part = 256
    parts = rows // part
    half, full = jnp.bfloat16, jnp.float32

    def keep_of(at):
        return jnp.where(at + lax.broadcasted_iota(jnp.int32, (part, 1), 0) < length, 1.0, 0.0)

    def core_copy(use, i):
        return pltpu.make_async_remote_copy(
            src_ref=send_p.at[i], dst_ref=recv_p.at[i], send_sem=psem.at[use, i], recv_sem=qsem.at[use, i],
            device_id=core, device_id_type=MESH,
        )

    def core_sent(use):
        for i in range(parts):
            core_copy(use, i).wait_send()
        if use < 2:
            pl.semaphore_signal(core_free, inc=1, device_id=core, device_id_type=MESH)
            pl.semaphore_wait(core_free, 1)

    def norm_parts(values):
        centred = values - jnp.mean(values, axis=1, keepdims=True)
        inverse = lax.rsqrt(jnp.mean(centred * centred, axis=1, keepdims=True) + epsilon)
        return centred * inverse, inverse

    def norm_grad(grad, normed, inverse, scale):
        hat = grad * scale
        middle = jnp.mean(hat, axis=1, keepdims=True)
        return inverse * (hat - middle - normed * jnp.mean(hat * normed, axis=1, keepdims=True))

    def run_ticks(first, last):
        lax.fori_loop(first, last, lambda i, _: (tick(i), 0)[1], 0)

    def mlp(vu, vd, cot, wide, hid, gp, gh, wsem, tsem, osem):
        loads = [pltpu.make_async_copy(a, b, wsem.at[n]) for n, (a, b) in enumerate(((wd, vd), (wu, vu)))]
        for x in loads:
            x.start()

        def tile(source, target, n, i):
            own = pl.ds(pl.multiple_of(i * part, part), part)
            slot = lax.rem(i, 2)
            return pltpu.make_async_copy(source.at[own, :], target.at[slot], tsem.at[n, slot])

        def stream(sources, i, body):
            for n, source, target in sources:
                tile(source, target, n, i).wait()

                @pl.when(i + 1 < parts)
                def _():
                    tile(source, target, n, i + 1).start()

            return body(i, pl.multiple_of(i * part, part), lax.rem(i, 2))

        def begin(sources):
            for n, source, target in sources:
                tile(source, target, n, jnp.int32(0)).start()

        streams = ((0, cotangent, cot), (1, slope, wide))
        begin(streams)
        left_loaded(0)
        run_ticks(0, 4)
        for x in loads:
            x.wait()

        def store_pre(i):
            own = pl.ds(pl.multiple_of(i * part, part), part)
            return pltpu.make_async_copy(gp, r_up.at[own, :], osem.at[0])

        def first(i, at, slot):
            x = (cot[slot].astype(full) * keep_of(at)).astype(half)
            g = mm_nt(x, vd[...]) * wide[slot].astype(full)

            @pl.when(i > 0)
            def _():
                store_pre(i - 1).wait()

            gp[...] = g.astype(half)
            store_pre(i).start()
            send_p[i] = mm_nt(gp[...], vu[...])
            core_copy(0, i).start()

            @pl.when(lax.rem(i, 2) == 1)
            def _():
                tick(4 + lax.div(i, 2))

            return 0

        lax.fori_loop(0, parts, lambda i, _: stream(streams, i, first), 0)
        store_pre(parts - 1).wait()
        streams_two = ((0, cotangent, cot), (2, hidden, hid))
        begin(streams_two)

        def store_hidden(i):
            own = pl.ds(pl.multiple_of(i * part, part), part)
            return pltpu.make_async_copy(gh, hidden_grad.at[own, :], osem.at[1])

        def second(i, at, slot, total):
            own = pl.ds(at, part)
            normed, inverse = norm_parts(hid[slot])
            turn(normed * scale_two[...], 1, own)
            core_copy(0, i).wait_recv()
            grad = send_p[i] + recv_p[i]

            @pl.when(i > 0)
            def _():
                store_hidden(i - 1).wait()

            gh[...] = cot[slot].astype(full) * keep_of(at) + norm_grad(grad, normed, inverse, scale_two[...])
            store_hidden(i).start()
            ga[own, :] = gh[...].astype(half)
            turn(gh[...], 2, own)
            return total + jnp.sum(grad * normed, axis=0, keepdims=True)

        term = lax.fori_loop(
            0, parts, lambda i, total: stream(streams_two, i, functools.partial(second, total=total)),
            jnp.zeros((1, width), full),
        )
        for j in range(8):
            terms[0, 8 + j : 9 + j, :] = term[:, 128 * j : 128 * j + 128]
        store_hidden(parts - 1).wait()
        core_sent(0)
        tick(jnp.int32(6))
        streams_three = ((1, r_down, wide),)
        begin(streams_three)

        def third(i, at, slot):
            send_p[i] = mm(wide[slot], vd[...])
            core_copy(1, i).start()
            return 0

        lax.fori_loop(0, parts, lambda i, _: stream(streams_three, i, third), 0)
        streams_four = ((2, hidden, hid),)
        begin(streams_four)
        tick(jnp.int32(7))

        def store_layer(i):
            own = pl.ds(pl.multiple_of(i * part, part), part)
            return pltpu.make_async_copy(cot.at[0], layer_out.at[own, :], osem.at[0])

        def fourth(i, at, slot):
            core_copy(1, i).wait_recv()

            @pl.when(i > 0)
            def _():
                store_layer(i - 1).wait()

            cot[0] = ((hid[slot] + (send_p[i] + recv_p[i])) * keep_of(at)).astype(half)
            store_layer(i).start()
            return 0

        lax.fori_loop(0, parts, lambda i, _: stream(streams_four, i, fourth), 0)
        store_layer(parts - 1).wait()
        core_sent(1)

    pl.run_scoped(
        mlp,
        pltpu.VMEM(wu.shape, half),
        pltpu.VMEM(wd.shape, half),
        pltpu.VMEM((2, part, width), half),
        pltpu.VMEM((2, part, slope.shape[1]), half),
        pltpu.VMEM((2, part, width), full),
        pltpu.VMEM((part, slope.shape[1]), half),
        pltpu.VMEM((part, width), full),
        pltpu.SemaphoreType.DMA((2,)),
        pltpu.SemaphoreType.DMA((3, 2)),
        pltpu.SemaphoreType.DMA((2,)),
    )

    def attention(q, k, v, o_t, lse, wm, cos, sin, bias, do, do_t, kh, vh, k_t, dq_t, asem):
        loads = [
            pltpu.make_async_copy(a, b, asem.at[n])
            for n, (a, b) in enumerate(
                ((q_in, q), (k_in, k), (v_in, v), (heads_t, o_t), (lse_in, lse), (merge_in, wm),
                 (cosine, cos), (sine, sin))
            )
        ]
        for x in loads:
            x.start()
        for x in loads:
            x.wait()
        place = lax.broadcasted_iota(jnp.int32, (rows, 128), 0)
        bias[...] = (jnp.where(place < length, 1.0, 0.0) - 1.0) * 1000000000.0
        lane = lax.broadcasted_iota(jnp.int32, (rows, 128), 1) < HEAD
        block = 256

        def unrotate_lanes(y):
            return (y * cos[...] - swap_halves(y) * sin[...]).astype(jnp.bfloat16)

        def pair(p, _):
            weight = wm[pl.ds(pl.multiple_of(128 * p, 128), 128), :]
            do[...] = mm_nt(ga[...], weight).astype(jnp.bfloat16)
            do_t[...] = mm_nt(weight, ga[...]).astype(jnp.bfloat16)
            k_t[...] = (k[p].astype(jnp.float32) * 0.125).T.astype(jnp.bfloat16)
            product_t = do_t[...].astype(jnp.float32) * o_t[p].astype(jnp.float32)
            dks, dvs = [], []
            for h in range(2):
                tick(8 + 2 * p + h)
                delta = jnp.sum(product_t[HEAD * h : HEAD * h + HEAD], axis=0, keepdims=True)
                own = lane == (h == 0)
                kh[...] = jnp.where(own, k[p].astype(jnp.float32) * 0.125, 0.0).astype(jnp.bfloat16)
                vh[...] = jnp.where(own, v[p].astype(jnp.float32), 0.0).astype(jnp.bfloat16)
                dk = jnp.zeros((rows, 128), jnp.float32)
                dv = jnp.zeros((rows, 128), jnp.float32)
                for b in range(0, rows, block):
                    cols = slice(b, b + block)
                    qb = q[p, cols, :]
                    s = mm_nt(kh[...], qb) + bias[:, :1]
                    soft = jnp.exp(s - lse[pl.ds(2 * p + h, 1), cols])
                    ds = soft * (mm(vh[...], do_t[:, cols]) - delta[:, cols])
                    ds = ds.astype(jnp.bfloat16)
                    dv = dv + mm(soft.astype(jnp.bfloat16), do[cols, :])
                    dk = dk + mm(ds, qb)
                    dq_t[HEAD * h : HEAD * h + HEAD, cols] = mm(k_t[HEAD * h : HEAD * h + HEAD, :], ds)
                dks.append(dk)
                dvs.append(dv)
            quad = 3 * lax.div(p, 2)
            at = pl.ds(pl.multiple_of(128 * lax.rem(p, 2), 128), 128)
            qkv[quad, :, at] = unrotate_lanes(dq_t[...].T)
            qkv[quad + 1, :, at] = unrotate_lanes(jnp.where(lane, dks[0], dks[1]) * 0.125)
            qkv[quad + 2, :, at] = jnp.where(lane, dvs[0], dvs[1]).astype(jnp.bfloat16)
            return 0

        lax.fori_loop(0, pairs, pair, 0)

    pl.run_scoped(
        attention,
        pltpu.VMEM((pairs, rows, 128), half),
        pltpu.VMEM((pairs, rows, 128), half),
        pltpu.VMEM((pairs, rows, 128), half),
        pltpu.VMEM((pairs, 128, rows), half),
        pltpu.VMEM((2 * pairs, rows), full),
        pltpu.VMEM(merge_in.shape, half),
        pltpu.VMEM((rows, 128), full),
        pltpu.VMEM((rows, 128), full),
        pltpu.VMEM((rows, 128), full),
        pltpu.VMEM((rows, 128), half),
        pltpu.VMEM((128, rows), half),
        pltpu.VMEM((rows, 128), half),
        pltpu.VMEM((rows, 128), half),
        pltpu.VMEM((128, rows), half),
        pltpu.VMEM((128, rows), full),
        pltpu.SemaphoreType.DMA((10,)),
    )

    def inner(vq, vk, vv, x_in, gh, to, sem, hsem, osem):
        loads = [
            pltpu.make_async_copy(a, b, sem.at[n])
            for n, (a, b) in enumerate(((wq, vq), (wk, vk), (wv, vv), (tokens, x_in)))
        ]
        for x in loads:
            x.start()
        for x in loads:
            x.wait()

        def send(i, _):
            at = pl.multiple_of(i * part, part)
            own = pl.ds(at, part)
            total = None
            for quad in range(2):
                for n, w in enumerate((vq, vk, vv)):
                    term = mm_nt(qkv[3 * quad + n, own, :], w[:, TILE * quad : TILE * quad + TILE])
                    total = term if total is None else total + term
            send_p[i] = total
            core_copy(2, i).start()
            normed, _ = norm_parts(x_in[own, :].astype(full) * keep_of(at))
            turn(normed * scale_one[...], 0, own)

            @pl.when(lax.rem(i, 2) == 1)
            def _():
                tick(16 + lax.div(i, 2))

            return 0

        lax.fori_loop(0, parts, send, 0)

        def store_tokens(i):
            own = pl.ds(pl.multiple_of(i * part, part), part)
            return pltpu.make_async_copy(to, tokens_out.at[own, :], osem)

        def take(i, total):
            at = pl.multiple_of(i * part, part)
            own = pl.ds(at, part)
            hidden_copy = pltpu.make_async_copy(hidden_grad.at[own, :], gh, hsem)
            hidden_copy.start()
            core_copy(2, i).wait_recv()
            grad = send_p[i] + recv_p[i]
            keep = keep_of(at)
            normed, inverse = norm_parts(x_in[own, :].astype(full) * keep)
            back = norm_grad(grad, normed, inverse, scale_one[...])
            hidden_copy.wait()

            @pl.when(i > 0)
            def _():
                store_tokens(i - 1).wait()

            to[...] = ((gh[...] + back) * keep).astype(half)
            store_tokens(i).start()
            return total + jnp.sum(grad * normed, axis=0, keepdims=True)

        first = lax.fori_loop(0, parts, take, jnp.zeros((1, width), full))
        store_tokens(parts - 1).wait()
        core_sent(2)
        for j in range(8):
            terms[0, j : j + 1, :] = first[:, 128 * j : 128 * j + 128]
        terms[0, 16:24, :] = jnp.broadcast_to(moment[...], (8, 128))

    pl.run_scoped(
        inner,
        pltpu.VMEM(wq.shape, half),
        pltpu.VMEM(wk.shape, half),
        pltpu.VMEM(wv.shape, half),
        pltpu.VMEM((rows, width), half),
        pltpu.VMEM((part, width), full),
        pltpu.VMEM((part, width), half),
        pltpu.SemaphoreType.DMA((4,)),
        pltpu.SemaphoreType.DMA,
        pltpu.SemaphoreType.DMA,
    )
    done = 18
    for stage in range(4):
        held = 2**stage
        exchange = pltpu.make_async_remote_copy(
            src_ref=terms.at[pl.ds(0, held)], dst_ref=terms.at[pl.ds(held, held)],
            send_sem=gsem.at[stage], recv_sem=jsem.at[stage], device_id=across(held), device_id_type=MESH,
        )
        exchange.start()
        tick(jnp.int32(done + stage))
        exchange.wait()
    rows_out[...] = terms[...]
    run_ticks(done + 4, ITEMS + LAGS[3])

    def drain(i, _):
        @pl.when(i >= ITEMS - RING)
        def _():
            copy(i, 0).wait_send()

        copy(i, 3).wait_send()
        return 0

    lax.fori_loop(0, ITEMS, drain, 0)


def backward(names, length, moment, scale_one, scale_two, *arrays):
    tokens, slope = arrays[-6], arrays[-4]
    rows, width = tokens.shape
    smem = pl.BlockSpec(memory_space=pltpu.SMEM)
    vmem = pl.BlockSpec(memory_space=pltpu.VMEM)
    hbm = pl.BlockSpec(memory_space=pl.ANY)
    half, full = jnp.bfloat16, jnp.float32
    dma = pltpu.SemaphoreType.DMA
    return pl.pallas_call(
        functools.partial(backward_kernel, names),
        out_shape=[
            jax.ShapeDtypeStruct((ITEMS, 64, TILE), full),
            jax.ShapeDtypeStruct((16, 24, 128), full),
            jax.ShapeDtypeStruct((rows, width), half),
            jax.ShapeDtypeStruct((rows, width), half),
            jax.ShapeDtypeStruct(slope.shape, half),
            jax.ShapeDtypeStruct((rows, width), full),
        ],
        in_specs=[smem] + [vmem] * 3 + [hbm] * len(arrays),
        out_specs=[vmem] * 2 + [hbm] * 4,
        scratch_shapes=[
            pltpu.VMEM((3, 16, 64, rows), half),
            pltpu.VMEM((RING, 8, 64, TILE), full),
            pltpu.VMEM((HELD, 8, 64, TILE), full),
            pltpu.VMEM((HELD, 4, 64, TILE), full),
            pltpu.VMEM((ITEMS, 2, 64, TILE), full),
            pltpu.VMEM((ITEMS, 1, 64, TILE), full),
            pltpu.VMEM((2, 2, rows, TILE), half),
            pltpu.VMEM((6, rows, TILE), half),
            pltpu.VMEM((rows // 256, 256, width), full),
            pltpu.VMEM((rows // 256, 256, width), full),
            pltpu.VMEM((rows, width), half),
            pltpu.VMEM((16, 24, 128), full),
            dma,
            dma((2, 2)),
            dma((4, ITEMS)),
            dma((4, ITEMS)),
            dma((3, 4)),
            dma((3, 4)),
            dma((4,)),
            dma((4,)),
            pltpu.SemaphoreType.REGULAR((3,)),
            pltpu.SemaphoreType.REGULAR((3,)),
            pltpu.SemaphoreType.REGULAR,
        ],
        compiler_params=pltpu.CompilerParams(
            collective_id=0, has_side_effects=True, vmem_limit_bytes=60 * 2**20
        ),
        name="backward",
    )(length, moment, scale_one, scale_two, *arrays)


def fast_body(
    tokens,
    cotangent,
    lengths,
    noise_times,
    query_weight,
    key_weight,
    value_weight,
    merge_weight,
    up_weight,
    down_weight,
    first_scales,
    second_scales,
):
    tokens, cotangent = tokens[0], cotangent[0]
    rows, width = tokens.shape
    table_rows = first_scales.shape[0]
    chunks = lax.axis_size("dp")
    names = ("dp", "tensor")
    moment = noise_times[0]
    scale_one = lax.dynamic_slice_in_dim(first_scales, moment, 1, axis=0)
    scale_two = lax.dynamic_slice_in_dim(second_scales, moment, 1, axis=0)
    cosine, sine = (jnp.asarray(a) for a in rope_lanes(rows))
    query, key, value, heads, heads_t, lse, hidden, activated, slope, mlp_t = forward(
        names, lengths, tokens, cotangent, scale_one, scale_two, cosine, sine,
        query_weight, key_weight, value_weight, merge_weight, up_weight,
    )
    pieces, gathered, grad_tokens, layer_output, _, _ = backward(
        names, lengths, jnp.full((1, 128), 1.0, jnp.float32) * moment.astype(jnp.float32), scale_one, scale_two,
        mlp_t, activated, heads, query, key, value, heads_t, lse, cosine, sine,
        merge_weight, query_weight, key_weight, value_weight, tokens, hidden, slope, cotangent, up_weight, down_weight,
    )
    wide = lambda a: a.transpose(1, 0, 2).reshape(width // chunks, -1)
    tall = lambda a: a.transpose(0, 2, 1).reshape(-1, width // chunks)
    grad_query, grad_key, grad_value = (wide(pieces[18 + k :: 3]) for k in range(3))
    hits = (gathered[:, 16, :1] == jnp.arange(table_rows, dtype=jnp.float32)[None, :]).astype(jnp.float32)
    mine = lax.axis_index("dp") * (width // chunks)
    terms = gathered[:, :16].reshape(chunks, 2, width)
    columns = lax.dynamic_slice_in_dim(terms, mine, width // chunks, axis=2).reshape(chunks, -1)
    tables = jnp.dot(hits.T, columns, precision=highest)
    grad_first, grad_second = jnp.split(tables, 2, axis=1)
    return (
        layer_output[None],
        grad_tokens[None],
        grad_query,
        grad_key,
        grad_value,
        tall(pieces[16:18]),
        wide(pieces[8:16]),
        tall(pieces[:8]),
        grad_first,
        grad_second,
    )


def body(
    tokens,
    cotangent,
    lengths,
    noise_times,
    query_weight,
    key_weight,
    value_weight,
    merge_weight,
    up_weight,
    down_weight,
    first_scales,
    second_scales,
):
    seq_count, length, width = tokens.shape
    local_width = query_weight.shape[1]
    local_heads = local_width // HEAD
    table_rows = first_scales.shape[0]
    flat_rows = seq_count * length
    scale_factor = 1.0 / math.sqrt(HEAD)
    block_rows = min(512, length)
    head_shape = (seq_count, length, local_heads, HEAD)
    row_mask = (jnp.arange(length, dtype=jnp.int32)[None, :] < lengths[:, None]).astype(jnp.float32)
    key_bias = (row_mask - 1.0) * 1000000000.0
    one_hot = (noise_times[:, None] == jnp.arange(table_rows, dtype=jnp.int32)[None, :]).astype(
        jnp.float32
    )
    scale_one = jnp.dot(one_hot, first_scales, precision=highest)
    scale_two = jnp.dot(one_hot, second_scales, precision=highest)
    cos_table, sin_table = rope_tables(length, HEAD)
    inputs = tokens.astype(jnp.float32) * row_mask[:, :, None]
    normed_one, inv_one = normalize(inputs)
    normal_in = (normed_one * scale_one[:, None, :]).astype(jnp.bfloat16).reshape(flat_rows, width)
    queries = jnp.dot(normal_in, query_weight, preferred_element_type=jnp.float32).reshape(
        head_shape
    )
    key_proj = jnp.dot(normal_in, key_weight, preferred_element_type=jnp.float32).reshape(
        head_shape
    )
    value_rows = (
        jnp.dot(normal_in, value_weight, preferred_element_type=jnp.float32)
        .astype(jnp.bfloat16)
        .reshape(head_shape)
    )
    query_rot = rotate(queries, cos_table, sin_table).astype(jnp.bfloat16)
    key_rot = rotate(key_proj, cos_table, sin_table).astype(jnp.bfloat16)
    attended = []
    log_sums = []
    for offset in range(0, length, block_rows):
        scores = block_scores(
            query_rot[:, offset : offset + block_rows], key_rot, key_bias, scale_factor
        )
        peak_score = jnp.max(scores, axis=-1, keepdims=True)
        exponent = jnp.exp(scores - peak_score)
        totals = jnp.sum(exponent, axis=-1, keepdims=True)
        soft_weights = (exponent / totals).astype(jnp.bfloat16)
        log_sums.append(peak_score + jnp.log(totals))
        attended.append(
            jnp.einsum(
                "shqk,skhd->sqhd", soft_weights, value_rows, preferred_element_type=jnp.float32
            )
        )
    heads_out = (
        jnp.concatenate(attended, axis=1).astype(jnp.bfloat16).reshape(flat_rows, local_width)
    )
    attn_part = jnp.dot(heads_out, merge_weight, preferred_element_type=jnp.float32)
    attn_total = lax.psum(attn_part, "tensor")
    hidden_one = inputs + attn_total.reshape(seq_count, length, width)
    normed_two, inv_two = normalize(hidden_one)
    normal_mid = (normed_two * scale_two[:, None, :]).astype(jnp.bfloat16).reshape(flat_rows, width)
    pre_act = jnp.dot(normal_mid, up_weight, preferred_element_type=jnp.float32)
    activated = gelu_tanh(pre_act).astype(jnp.bfloat16)
    mlp_part = jnp.dot(activated, down_weight, preferred_element_type=jnp.float32)
    mlp_total = lax.psum(mlp_part, "tensor")
    layer_output = (
        (hidden_one + mlp_total.reshape(seq_count, length, width)) * row_mask[:, :, None]
    ).astype(jnp.bfloat16)
    grad_final = cotangent.astype(jnp.float32) * row_mask[:, :, None]
    grad_mlp = grad_final.astype(jnp.bfloat16).reshape(flat_rows, width)
    grad_down = jnp.dot(activated.T, grad_mlp, preferred_element_type=jnp.float32)
    grad_act = jnp.dot(grad_mlp, down_weight.T, preferred_element_type=jnp.float32)
    unused_value, gelu_back = jax.vjp(gelu_tanh, pre_act)
    grad_pre = gelu_back(grad_act)[0].astype(jnp.bfloat16)
    grad_up = jnp.dot(normal_mid.T, grad_pre, preferred_element_type=jnp.float32)
    mid_part = jnp.dot(grad_pre, up_weight.T, preferred_element_type=jnp.float32)
    grad_mid = lax.psum(mid_part, "tensor").reshape(seq_count, length, width)
    grad_hat_two, scale_grad_two = norm_back(grad_mid, normed_two, inv_two, scale_two)
    grad_hidden = grad_final + grad_hat_two
    grad_second = jnp.dot(one_hot.T, scale_grad_two, precision=highest)
    grad_attn = grad_hidden.astype(jnp.bfloat16).reshape(flat_rows, width)
    grad_merge = jnp.dot(heads_out.T, grad_attn, preferred_element_type=jnp.float32)
    grad_heads = (
        jnp.dot(grad_attn, merge_weight.T, preferred_element_type=jnp.float32)
        .astype(jnp.bfloat16)
        .reshape(head_shape)
    )
    grad_keys = jnp.zeros(head_shape, jnp.float32)
    grad_values = jnp.zeros(head_shape, jnp.float32)
    query_grads = []
    for block_index in range(len(log_sums)):
        offset = block_index * block_rows
        query_block = query_rot[:, offset : offset + block_rows]
        grad_block = grad_heads[:, offset : offset + block_rows]
        scores = block_scores(query_block, key_rot, key_bias, scale_factor)
        soft_weights = jnp.exp(scores - log_sums[block_index])
        grad_soft = jnp.einsum(
            "sqhd,skhd->shqk", grad_block, value_rows, preferred_element_type=jnp.float32
        )
        grad_values = grad_values + jnp.einsum(
            "shqk,sqhd->skhd",
            soft_weights.astype(jnp.bfloat16),
            grad_block,
            preferred_element_type=jnp.float32,
        )
        grad_scores = (
            soft_weights * (grad_soft - jnp.sum(soft_weights * grad_soft, axis=-1, keepdims=True))
        ).astype(jnp.bfloat16)
        query_grads.append(
            jnp.einsum("shqk,skhd->sqhd", grad_scores, key_rot, preferred_element_type=jnp.float32)
            * scale_factor
        )
        grad_keys = (
            grad_keys
            + jnp.einsum(
                "shqk,sqhd->skhd", grad_scores, query_block, preferred_element_type=jnp.float32
            )
            * scale_factor
        )
    query_back = (
        unrotate(jnp.concatenate(query_grads, axis=1), cos_table, sin_table)
        .astype(jnp.bfloat16)
        .reshape(flat_rows, local_width)
    )
    key_back = (
        unrotate(grad_keys, cos_table, sin_table)
        .astype(jnp.bfloat16)
        .reshape(flat_rows, local_width)
    )
    value_back = grad_values.astype(jnp.bfloat16).reshape(flat_rows, local_width)
    grad_query = jnp.dot(normal_in.T, query_back, preferred_element_type=jnp.float32)
    grad_key = jnp.dot(normal_in.T, key_back, preferred_element_type=jnp.float32)
    grad_value = jnp.dot(normal_in.T, value_back, preferred_element_type=jnp.float32)
    inner_part = jnp.dot(query_back, query_weight.T, preferred_element_type=jnp.float32)
    inner_part = inner_part + jnp.dot(key_back, key_weight.T, preferred_element_type=jnp.float32)
    inner_part = inner_part + jnp.dot(
        value_back, value_weight.T, preferred_element_type=jnp.float32
    )
    grad_inner = lax.psum(inner_part, "tensor").reshape(seq_count, length, width)
    grad_hat_one, scale_grad_one = norm_back(grad_inner, normed_one, inv_one, scale_one)
    grad_tokens = ((grad_hidden + grad_hat_one) * row_mask[:, :, None]).astype(jnp.bfloat16)
    grad_first = jnp.dot(one_hot.T, scale_grad_one, precision=highest)
    summed = (
        lax.psum_scatter(grad_query, "dp", scatter_dimension=0, tiled=True),
        lax.psum_scatter(grad_key, "dp", scatter_dimension=0, tiled=True),
        lax.psum_scatter(grad_value, "dp", scatter_dimension=0, tiled=True),
        lax.psum_scatter(grad_merge, "dp", scatter_dimension=1, tiled=True),
        lax.psum_scatter(grad_up, "dp", scatter_dimension=0, tiled=True),
        lax.psum_scatter(grad_down, "dp", scatter_dimension=1, tiled=True),
        lax.psum_scatter(grad_first, "dp", scatter_dimension=1, tiled=True),
        lax.psum_scatter(grad_second, "dp", scatter_dimension=1, tiled=True),
    )
    return (
        layer_output,
        grad_tokens,
        summed[0],
        summed[1],
        summed[2],
        summed[3],
        summed[4],
        summed[5],
        summed[6],
        summed[7],
    )


def solution(mesh):
    fast = mesh.shape["dp"] == 16 and mesh.shape["tensor"] == 2
    return jax.shard_map(
        fast_body if fast else body,
        mesh=mesh,
        in_specs=(
            P("dp", None, None),
            P("dp", None, None),
            P("dp"),
            P("dp"),
            P(None, "tensor"),
            P(None, "tensor"),
            P(None, "tensor"),
            P("tensor", None),
            P(None, "tensor"),
            P("tensor", None),
            P(),
            P(),
        ),
        out_specs=(
            P("dp", None, None),
            P("dp", None, None),
            P("dp", "tensor"),
            P("dp", "tensor"),
            P("dp", "tensor"),
            P("tensor", "dp"),
            P("dp", "tensor"),
            P("tensor", "dp"),
            P(None, "dp"),
            P(None, "dp"),
        ),
        check_vma=False,
    )
```

profile of v0, /device:TPU:0, one launch (start us, length us, event | category | flops | bytes accessed | tf_op | source)
XLA Modules:
  0.0 287.5 jit_solution(18080144844424341038)
XLA Ops:
  1.3 1.4 constant_dynamic-slice_fusion.1
  3.3 44.9 %forward.1 = (bf16[4,1024,128]{2,1,0:T(8,128)(2,1)}, bf16[4,1024,128]{2,1,0:T(8,128)(2,1)}, bf16[4,1024,128]{2,1,0:T(8,128)(2,1)}, bf16[4,1024,128]{2,1,0:T(8,12...) custom-call(s32[1]{0:T(128)S(6)} %copy.38.length_ref, ...), custom_call_target="tpu_custom_call" | custom-call | tf_op jit(solution)/shard_map/forward/pallas_call | solution.py:270
  48.2 0.5 mul.6.moment
  48.7 225.2 %backward.1 = (f32[24,64,256]{2,1,0:T(8,128)}, f32[16,24,128]{2,1,0:T(8,128)}, bf16[1024,1024]{1,0:T(8,128)(2,1)}, bf16[1024,1024]{1,0:T(8,128)(2,1)}, bf16[1024,2048]{1,0:T(8,128)(2,1)}, /*index=5*/f32[1024,1024]{1,0:T(8,128)}) custom-call(s32[1]{0:T(128)S(6)} %copy.38.length_ref, f32[1,128]{1,0:T(1,128)} %mul.6.moment, ...), custom_call_target="tpu_custom_call" | custom-call | tf_op jit(solution)/shard_map/backward/pallas_call | solution.py:852
  273.9 0.9 slice.31
  274.9 0.1 reshape.51
  274.9 0.1 constant_dynamic-slice_fusion
  275.0 0.1 reshape.52
  275.1 1.0 slice_reduce_fusion
  276.1 0.3 fusion
  276.4 0.7 fusion.2
  277.1 1.3 slice_bitcast_fusion
  278.4 0.0 copy-start.1
  278.4 0.8 copy.34
  279.2 0.8 copy.35
  280.1 1.1 slice_bitcast_fusion.2
  281.2 0.7 copy.30
  281.9 0.7 copy.31
  282.5 0.7 copy.32
  283.2 0.7 copy.33
  283.9 0.0 copy-done.1
  283.9 0.0 copy-start
  283.9 1.3 copy.40
  285.2 1.0 copy-done
  286.2 1.3 copy.41
Async XLA Ops:
  278.4 5.5 %copy-start.1 = (bf16[1024,1024]{1,0:T(8,128)(2,1)S(1)}, bf16[1024,1024]{1,0:T(8,128)(2,1)}, u32[]{:S(2)}) copy-start(bf16[1024,1024]{1,0:T(8,128)(2,1)} %get-tuple-element.34) | copy-start | bytes 6291460
  283.9 2.3 copy-start
where the time goes:
time: 288 us
  Pallas kernels  270 us (94%)
  local copies, waits for them, and re-layouts  15.2 us (5%)
    pallas_call x1, Pallas kernels, backward(): pl.pallas_call(functools.partial(backward_kernel, names), out_shape=[jax....  225 us
    pallas_call x1, Pallas kernels, forward(): pl.pallas_call(functools.partial(forward_kernel, names), out_shape=[jax.S...  44.9 us
    unnamed x8, local copies, waits for them, and re-layouts  6.09 us

commit v1 on v0

--- a/solution.py
+++ b/solution.py
@@ -122,9 +122,10 @@
 
 
 def forward_kernel(
-    names, length_ref, tokens, cotangent, scale_one, scale_two, cosine, sine, wq, wk, wv, wm, wu,
-    q_out, k_out, v_out, heads, heads_t, lse, hidden, act, slope, mlp_t,
-    nin, vq, vk, vv, vm, vu, other_m, v_t, send_m, recv_m, send_o, recv_o, bias, wsem, ssem, rsem,
+    names, length_ref, tokens, scale_one, scale_two, cotangent_in, cosine_in, sine_in, wq, wk, wv, wm,
+    q_hbm, k_hbm, v_hbm, heads_hbm, heads_t_hbm, lse_hbm, hidden_hbm, mid_hbm, mlp_t_hbm,
+    q_out, k_out, v_out, heads, heads_t, lse, hidden, mid, mlp_t, cotangent, cosine, sine,
+    nin, vq, vk, vv, vm, other_m, v_t, send_m, recv_m, send_o, recv_o, bias, wsem, osem, tsem, ssem, rsem,
 ):
     rows, width = tokens.shape
     pairs = q_out.shape[0]
@@ -133,7 +134,9 @@
     other = tuple(other[n] for n in names)
     loads = [
         pltpu.make_async_copy(a, b, wsem.at[i])
-        for i, (a, b) in enumerate(((wq, vq), (wk, vk), (wv, vv), (wm, vm), (wu, vu)))
+        for i, (a, b) in enumerate(
+            ((wq, vq), (wk, vk), (wv, vv), (cosine_in, cosine), (sine_in, sine), (wm, vm), (cotangent_in, cotangent))
+        )
     ]
     for c in loads:
         c.start()
@@ -157,7 +160,7 @@
         return 0
 
     lax.fori_loop(0, rows // 128, norm_rows, 0)
-    for c in loads[:4]:
+    for c in loads:
         c.wait()
     send_m[...] = vm[...].astype(jnp.float32)
     merge_copy = pltpu.make_async_remote_copy(
@@ -184,6 +187,15 @@
         return 0
 
     lax.fori_loop(0, rows // 256, project, 0)
+    stores = [
+        pltpu.make_async_copy(a, b, osem.at[i])
+        for i, (a, b) in enumerate(
+            ((q_out, q_hbm), (k_out, k_hbm), (v_out, v_hbm), (heads, heads_hbm), (heads_t, heads_t_hbm), (lse, lse_hbm),
+             (mlp_t, mlp_t_hbm))
+        )
+    ]
+    for c in stores[:3]:
+        c.start()
 
     def o_copy(p):
         return pltpu.make_async_remote_copy(
@@ -218,11 +230,19 @@
         return 0
 
     lax.fori_loop(0, pairs, attend, 0)
+    for c in stores[3:]:
+        c.start()
     merge_copy.wait()
     other_m[...] = recv_m[...].astype(jnp.bfloat16)
     for p in range(pairs):
         o_copy(p).wait()
-    loads[4].wait()
+
+    def tile_stores(i):
+        own = pl.ds(pl.multiple_of(i * 256, 256), 256)
+        return [
+            pltpu.make_async_copy(hidden.at[own, :], hidden_hbm.at[own, :], tsem.at[0, i]),
+            pltpu.make_async_copy(mid.at[own, :], mid_hbm.at[own, :], tsem.at[1, i]),
+        ]
 
     def finish(i, _):
         at = pl.multiple_of(i * 256, 256)
@@ -232,24 +252,22 @@
         attn = mm(mine, vm[...]) + mm(theirs, other_m[...])
         one = tokens[own, :].astype(jnp.float32) * mask_of(at, 256) + attn
         hidden[own, :] = one
-        normal = (centre(one) * scale_two[...]).astype(jnp.bfloat16)
-        for j in range(0, vu.shape[1], 512):
-            v = mm(normal, vu[:, j : j + 512])
-            square = v * v
-            t = jnp.tanh(0.7978845608028654 * v * (1.0 + 0.044715 * square))
-            up = 0.5 * (1.0 + t)
-            act[own, j : j + 512] = (v * up).astype(jnp.bfloat16)
-            slope[own, j : j + 512] = (
-                up + 0.5 * v * (1.0 - t * t) * (0.7978845608028654 * (1.0 + 0.134145 * square))
-            ).astype(jnp.bfloat16)
+        mid[own, :] = (centre(one) * scale_two[...]).astype(jnp.bfloat16)
+        for c in tile_stores(i):
+            c.start()
         return 0
 
     lax.fori_loop(0, rows // 256, finish, 0)
-
-
-def forward(names, length, tokens, cotangent, scale_one, scale_two, cosine, sine, wq, wk, wv, wm, wu):
+    for c in stores:
+        c.wait()
+    for i in range(rows // 256):
+        for c in tile_stores(i):
+            c.wait()
+
+
+def forward(names, length, tokens, scale_one, scale_two, cotangent, cosine, sine, wq, wk, wv, wm):
     rows, width = tokens.shape
-    local, units = wq.shape[1], wu.shape[1]
+    local = wq.shape[1]
     pairs = local // 128
     vmem = pl.BlockSpec(memory_space=pltpu.VMEM)
     hbm = pl.BlockSpec(memory_space=pl.ANY)
@@ -263,22 +281,24 @@
         ((pairs, 128, rows), half),
         ((2 * pairs, rows), full),
         ((rows, width), full),
-        ((rows, units), half),
-        ((rows, units), half),
+        ((rows, width), half),
         ((16, width // 16, rows), half),
     ]
     return pl.pallas_call(
         functools.partial(forward_kernel, names),
         out_shape=[jax.ShapeDtypeStruct(*s) for s in shapes],
-        in_specs=[pl.BlockSpec(memory_space=pltpu.SMEM)] + [vmem] * 6 + [hbm] * 5,
-        out_specs=[vmem] * len(shapes),
-        scratch_shapes=[
+        in_specs=[pl.BlockSpec(memory_space=pltpu.SMEM)] + [vmem] * 3 + [hbm] * 7,
+        out_specs=[hbm] * len(shapes),
+        scratch_shapes=[pltpu.VMEM(*s) for s in shapes]
+        + [
+            pltpu.VMEM((rows, width), half),
+            pltpu.VMEM((rows, 128), full),
+            pltpu.VMEM((rows, 128), full),
             pltpu.VMEM((rows, width), half),
             pltpu.VMEM(wq.shape, half),
             pltpu.VMEM(wk.shape, half),
             pltpu.VMEM(wv.shape, half),
             pltpu.VMEM(wm.shape, half),
-            pltpu.VMEM(wu.shape, half),
             pltpu.VMEM(wm.shape, half),
             pltpu.VMEM((pairs, 128, rows), half),
             pltpu.VMEM(wm.shape, full),
@@ -286,20 +306,22 @@
             pltpu.VMEM((pairs, rows, 128), full),
             pltpu.VMEM((pairs, rows, 128), full),
             pltpu.VMEM((rows, 128), full),
-            pltpu.SemaphoreType.DMA((5,)),
+            pltpu.SemaphoreType.DMA((7,)),
+            pltpu.SemaphoreType.DMA((7,)),
+            pltpu.SemaphoreType.DMA((2, 4)),
             pltpu.SemaphoreType.DMA((1 + pairs,)),
             pltpu.SemaphoreType.DMA((1 + pairs,)),
         ],
         compiler_params=pltpu.CompilerParams(collective_id=1, has_side_effects=True, vmem_limit_bytes=58 * 2**20),
         name="forward",
-    )(length, tokens, cotangent, scale_one, scale_two, cosine, sine, wq, wk, wv, wm, wu)
+    )(length, tokens, scale_one, scale_two, cotangent, cosine, sine, wq, wk, wv, wm)
 
 
 ITEMS = 24
 TILE = 256
 RING = 5
 HELD = 12
-LAGS = (4, 7, 9, 11)
+LAGS = (4, 6, 8, 10)
 FIRSTS = (0, 8, 16, 18, 24)
 
 
@@ -320,7 +342,8 @@
 
 
 def color_of(i):
-    return lax.rem(lax.rem(i, 8), 3)
+    turn = i - lax.div(i + 2, 5)
+    return jnp.where(lax.rem(i, 5) == 2, 2, lax.rem(turn, 2))
 
 
 def slot_of(i):
@@ -329,9 +352,9 @@
 
 def backward_kernel(
     names, length_ref, moment, scale_one, scale_two,
-    l_down, r_down, heads, q_in, k_in, v_in, heads_t, lse_in, cosine, sine,
-    merge_in, wq, wk, wv, tokens, hidden, slope, cotangent, wu, wd,
-    out, rows_out, tokens_out, layer_out, r_up, hidden_grad,
+    l_down, mid_in, heads, q_in, k_in, v_in, heads_t, lse_in, cosine, sine,
+    merge_in, wq, wk, wv, tokens, hidden, cotangent, wu, wd,
+    out, rows_out, tokens_out, layer_out, r_down, slope, r_up, hidden_grad,
     left, s1, r1, r2, r3, r4, rb, qkv, send_p, recv_p, ga, terms,
     lsem, fsem, ssem, csem, psem, qsem, gsem, jsem, credit, credit_two, core_free,
 ):
@@ -417,25 +440,6 @@
         )
 
     def tick(i):
-        @pl.when(i < ITEMS)
-        def _():
-            @pl.when(i >= RING)
-            def _():
-                copy(i - RING, 0).wait_send()
-
-            fetched(i, 0)
-            s1[lax.rem(i, RING)] = product(i, 1, 0)
-
-            @pl.when(i >= HELD)
-            def _():
-                pl.semaphore_wait(credit.at[color_of(i)], 1)
-
-            copy(i, 0).start()
-
-            @pl.when((i + 2 < ITEMS))
-            def _():
-                fetch(i + 2, 0)
-
         a = i - LAGS[0]
 
         @pl.when((a >= 0) & (a < ITEMS))
@@ -493,9 +497,28 @@
             copy(e, 3).wait_recv()
             out[e] = r4[e, 0] + r3[e, 0]
 
-    for lane in range(2):
-        fetch(jnp.int32(0), lane)
-        fetch(jnp.int32(1), lane)
+        @pl.when(i < ITEMS)
+        def _():
+            @pl.when(i >= RING)
+            def _():
+                copy(i - RING, 0).wait_send()
+
+            @pl.when(i >= LAGS[0])
+            def _():
+                fetched(i, 0)
+
+            s1[lax.rem(i, RING)] = product(i, 1, 0)
+
+            @pl.when(i >= HELD)
+            def _():
+                pl.semaphore_wait(credit.at[color_of(i)], 1)
+
+            copy(i, 0).start()
+
+            @pl.when((i + 2 < ITEMS) & (i >= LAGS[0]))
+            def _():
+                fetch(i + 2, 0)
+
     rows, width = tokens.shape
     pairs = q_in.shape[0]
     length = length_ref[0]
@@ -532,10 +555,49 @@
     def run_ticks(first, last):
         lax.fori_loop(first, last, lambda i, _: (tick(i), 0)[1], 0)
 
-    def mlp(vu, vd, cot, wide, hid, gp, gh, wsem, tsem, osem):
-        loads = [pltpu.make_async_copy(a, b, wsem.at[n]) for n, (a, b) in enumerate(((wd, vd), (wu, vu)))]
-        for x in loads:
-            x.start()
+    def mlp(vu, vd, cot, wide, hid, gp, gh, wsem, usem, dsem, tsem, osem):
+        mid_load = pltpu.make_async_copy(mid_in, ga, wsem.at[0])
+        mid_load.start()
+        tiles = wu.shape[1] // TILE
+
+        def columns(k):
+            return pl.ds(pl.multiple_of(k * TILE, TILE), TILE)
+
+        def up_load(k):
+            return pltpu.make_async_copy(wu.at[:, columns(k)], vu.at[:, columns(k)], usem.at[k])
+
+        for k in range(tiles):
+            up_load(k).start()
+        down_load = pltpu.make_async_copy(wd, vd, wsem.at[1])
+        down_load.start()
+
+        def tile_stores(k, lane):
+            slot = lax.rem(k, 2)
+            return (
+                pltpu.make_async_copy(rb.at[lane, slot], r_down.at[:, columns(k)], dsem.at[0, slot]),
+                pltpu.make_async_copy(qkv.at[slot], slope.at[:, columns(k)], dsem.at[1, slot]),
+            )
+
+        def up_tile(k, lane):
+            slot = lax.rem(k, 2)
+
+            @pl.when(k >= 2)
+            def _():
+                for x in tile_stores(k - 2, lane):
+                    x.wait()
+
+            up_load(k).wait()
+            for r in range(0, rows, 512):
+                v = mm(ga[r : r + 512, :], vu[:, columns(k)])
+                square = v * v
+                t = jnp.tanh(0.7978845608028654 * v * (1.0 + 0.044715 * square))
+                above = 0.5 * (1.0 + t)
+                rb[lane, slot, r : r + 512, :] = (v * above).astype(half)
+                qkv[slot, r : r + 512, :] = (
+                    above + 0.5 * v * (1.0 - t * t) * (0.7978845608028654 * (1.0 + 0.134145 * square))
+                ).astype(half)
+            for x in tile_stores(k, lane):
+                x.start()
 
         def tile(source, target, n, i):
             own = pl.ds(pl.multiple_of(i * part, part), part)
@@ -556,12 +618,25 @@
             for n, source, target in sources:
                 tile(source, target, n, jnp.int32(0)).start()
 
+        mid_load.wait()
+        left_loaded(0)
+
+        def early(k, _):
+            up_tile(k, 0)
+            tick(k)
+            return 0
+
+        lax.fori_loop(0, LAGS[0], early, 0)
+        lax.fori_loop(LAGS[0], tiles, lambda k, _: (up_tile(k, 1), 0)[1], 0)
+        for k in (tiles - 2, tiles - 1):
+            for x in tile_stores(k, 1):
+                x.wait()
+        for i in range(2):
+            fetch(jnp.int32(i), 1)
+            fetch(jnp.int32(LAGS[0] + i), 0)
         streams = ((0, cotangent, cot), (1, slope, wide))
         begin(streams)
-        left_loaded(0)
-        run_ticks(0, 4)
-        for x in loads:
-            x.wait()
+        down_load.wait()
 
         def store_pre(i):
             own = pl.ds(pl.multiple_of(i * part, part), part)
@@ -580,14 +655,15 @@
             send_p[i] = mm_nt(gp[...], vu[...])
             core_copy(0, i).start()
 
-            @pl.when(lax.rem(i, 2) == 1)
-            def _():
-                tick(4 + lax.div(i, 2))
+            @pl.when(i < 2)
+            def _():
+                tick(LAGS[0] + i)
 
             return 0
 
         lax.fori_loop(0, parts, lambda i, _: stream(streams, i, first), 0)
         store_pre(parts - 1).wait()
+        run_ticks(LAGS[0] + 2, LAGS[0] + 4)
         streams_two = ((0, cotangent, cot), (2, hidden, hid))
         begin(streams_two)
 
@@ -620,7 +696,6 @@
             terms[0, 8 + j : 9 + j, :] = term[:, 128 * j : 128 * j + 128]
         store_hidden(parts - 1).wait()
         core_sent(0)
-        tick(jnp.int32(6))
         streams_three = ((1, r_down, wide),)
         begin(streams_three)
 
@@ -632,7 +707,7 @@
         lax.fori_loop(0, parts, lambda i, _: stream(streams_three, i, third), 0)
         streams_four = ((2, hidden, hid),)
         begin(streams_four)
-        tick(jnp.int32(7))
+        tick(jnp.int32(LAGS[0] + 4))
 
         def store_layer(i):
             own = pl.ds(pl.multiple_of(i * part, part), part)
@@ -658,11 +733,13 @@
         pltpu.VMEM(wu.shape, half),
         pltpu.VMEM(wd.shape, half),
         pltpu.VMEM((2, part, width), half),
-        pltpu.VMEM((2, part, slope.shape[1]), half),
+        pltpu.VMEM((2, part, wu.shape[1]), half),
         pltpu.VMEM((2, part, width), full),
-        pltpu.VMEM((part, slope.shape[1]), half),
+        pltpu.VMEM((part, wu.shape[1]), half),
         pltpu.VMEM((part, width), full),
         pltpu.SemaphoreType.DMA((2,)),
+        pltpu.SemaphoreType.DMA((wu.shape[1] // TILE,)),
+        pltpu.SemaphoreType.DMA((2, 2)),
         pltpu.SemaphoreType.DMA((3, 2)),
         pltpu.SemaphoreType.DMA((2,)),
     )
@@ -695,7 +772,7 @@
             product_t = do_t[...].astype(jnp.float32) * o_t[p].astype(jnp.float32)
             dks, dvs = [], []
             for h in range(2):
-                tick(8 + 2 * p + h)
+                tick(LAGS[0] + 5 + 2 * p + h)
                 delta = jnp.sum(product_t[HEAD * h : HEAD * h + HEAD], axis=0, keepdims=True)
                 own = lane == (h == 0)
                 kh[...] = jnp.where(own, k[p].astype(jnp.float32) * 0.125, 0.0).astype(jnp.bfloat16)
@@ -766,9 +843,9 @@
             normed, _ = norm_parts(x_in[own, :].astype(full) * keep_of(at))
             turn(normed * scale_one[...], 0, own)
 
-            @pl.when(lax.rem(i, 2) == 1)
-            def _():
-                tick(16 + lax.div(i, 2))
+            @pl.when(i == 1)
+            def _():
+                tick(LAGS[0] + 13)
 
             return 0
 
@@ -783,6 +860,11 @@
             own = pl.ds(at, part)
             hidden_copy = pltpu.make_async_copy(hidden_grad.at[own, :], gh, hsem)
             hidden_copy.start()
+
+            @pl.when(i < 2)
+            def _():
+                tick(LAGS[0] + 14 + i)
+
             core_copy(2, i).wait_recv()
             grad = send_p[i] + recv_p[i]
             keep = keep_of(at)
@@ -817,7 +899,7 @@
         pltpu.SemaphoreType.DMA,
         pltpu.SemaphoreType.DMA,
     )
-    done = 18
+    done = LAGS[0] + 16
     for stage in range(4):
         held = 2**stage
         exchange = pltpu.make_async_remote_copy(
@@ -842,7 +924,7 @@
 
 
 def backward(names, length, moment, scale_one, scale_two, *arrays):
-    tokens, slope = arrays[-6], arrays[-4]
+    tokens, up = arrays[-5], arrays[-2]
     rows, width = tokens.shape
     smem = pl.BlockSpec(memory_space=pltpu.SMEM)
     vmem = pl.BlockSpec(memory_space=pltpu.VMEM)
@@ -856,11 +938,13 @@
             jax.ShapeDtypeStruct((16, 24, 128), full),
             jax.ShapeDtypeStruct((rows, width), half),
             jax.ShapeDtypeStruct((rows, width), half),
-            jax.ShapeDtypeStruct(slope.shape, half),
+            jax.ShapeDtypeStruct((rows, up.shape[1]), half),
+            jax.ShapeDtypeStruct((rows, up.shape[1]), half),
+            jax.ShapeDtypeStruct((rows, up.shape[1]), half),
             jax.ShapeDtypeStruct((rows, width), full),
         ],
         in_specs=[smem] + [vmem] * 3 + [hbm] * len(arrays),
-        out_specs=[vmem] * 2 + [hbm] * 4,
+        out_specs=[vmem] * 2 + [hbm] * 6,
         scratch_shapes=[
             pltpu.VMEM((3, 16, 64, rows), half),
             pltpu.VMEM((RING, 8, 64, TILE), full),
@@ -893,6 +977,74 @@
     )(length, moment, scale_one, scale_two, *arrays)
 
 
+def finish_kernel(
+    names, pieces, gathered, tokens_in, layer_in,
+    layer_out, tokens_out, grad_q, grad_k, grad_v, grad_m, grad_u, grad_d, first, second, held, sem,
+):
+    parts = held.shape[1]
+    step = layer_in.shape[0] // parts
+
+    def move(n, k):
+        source, target = ((layer_in, layer_out), (tokens_in, tokens_out))[n]
+        own = pl.ds(k * step, step)
+        return (
+            pltpu.make_async_copy(source.at[own, :], held.at[n, k], sem.at[0, n, k]),
+            pltpu.make_async_copy(held.at[n, k], target.at[own, :], sem.at[1, n, k]),
+        )
+
+    moves = [move(n, k) for n in range(2) for k in range(parts)]
+    for m in moves:
+        m[0].start()
+    for k in range(8):
+        grad_d[:, TILE * k : TILE * k + TILE] = pieces[k]
+        grad_u[:, TILE * k : TILE * k + TILE] = pieces[8 + k]
+    for k in range(2):
+        grad_m[:, TILE * k : TILE * k + TILE] = pieces[16 + k]
+        for n, ref in enumerate((grad_q, grad_k, grad_v)):
+            ref[:, TILE * k : TILE * k + TILE] = pieces[18 + 3 * k + n]
+    for m in moves:
+        m[0].wait()
+        m[1].start()
+    d = lax.axis_index(names[0])
+    count, table_rows = first.shape
+    upper = lax.rem(d, 2) == 1
+    places = lax.broadcasted_iota(jnp.int32, (table_rows, 128), 0).astype(jnp.float32)
+    total = jnp.zeros((table_rows, 128), jnp.float32)
+    for s in range(gathered.shape[0]):
+        row = []
+        for base in (0, 8):
+            part = gathered[s, pl.ds(base + lax.div(d, 2), 1), :]
+            row.append(jnp.where(upper, part[:, count:], part[:, :count]))
+        total = total + jnp.where(places == gathered[s, 16:17, :], jnp.concatenate(row, axis=1), 0.0)
+    turned = total.T
+    first[...] = turned[:count]
+    second[...] = turned[count:]
+    for m in moves:
+        m[1].wait()
+
+
+def finish(names, table_rows, pieces, gathered, tokens, layer):
+    vmem = pl.BlockSpec(memory_space=pltpu.VMEM)
+    hbm = pl.BlockSpec(memory_space=pl.ANY)
+    full = jnp.float32
+    rows, width = layer.shape
+    shapes = [(64, 512)] * 4 + [(64, 2048), (64, 2048), (64, table_rows), (64, table_rows)]
+    layer, tokens, *grads = pl.pallas_call(
+        functools.partial(finish_kernel, names),
+        out_shape=[jax.ShapeDtypeStruct(a.shape, a.dtype) for a in (layer, tokens)]
+        + [jax.ShapeDtypeStruct(s, full) for s in shapes],
+        in_specs=[vmem] * 2 + [hbm] * 2,
+        out_specs=[hbm] * 2 + [vmem] * len(shapes),
+        scratch_shapes=[
+            pltpu.VMEM((2, 4, rows // 4, width), layer.dtype),
+            pltpu.SemaphoreType.DMA((2, 2, 4)),
+        ],
+        name="finish",
+    )(pieces, gathered, tokens, layer)
+    query, key, value, merge, up, down, first, second = grads
+    return layer[None], tokens[None], query, key, value, merge.T, up, down.T, first.T, second.T
+
+
 def fast_body(
     tokens,
     cotangent,
@@ -909,43 +1061,21 @@
 ):
     tokens, cotangent = tokens[0], cotangent[0]
     rows, width = tokens.shape
-    table_rows = first_scales.shape[0]
-    chunks = lax.axis_size("dp")
     names = ("dp", "tensor")
     moment = noise_times[0]
     scale_one = lax.dynamic_slice_in_dim(first_scales, moment, 1, axis=0)
     scale_two = lax.dynamic_slice_in_dim(second_scales, moment, 1, axis=0)
     cosine, sine = (jnp.asarray(a) for a in rope_lanes(rows))
-    query, key, value, heads, heads_t, lse, hidden, activated, slope, mlp_t = forward(
-        names, lengths, tokens, cotangent, scale_one, scale_two, cosine, sine,
-        query_weight, key_weight, value_weight, merge_weight, up_weight,
-    )
-    pieces, gathered, grad_tokens, layer_output, _, _ = backward(
+    query, key, value, heads, heads_t, lse, hidden, normal_mid, mlp_t = forward(
+        names, lengths, tokens, scale_one, scale_two, cotangent, cosine, sine,
+        query_weight, key_weight, value_weight, merge_weight,
+    )
+    pieces, gathered, grad_tokens, layer_output, *_ = backward(
         names, lengths, jnp.full((1, 128), 1.0, jnp.float32) * moment.astype(jnp.float32), scale_one, scale_two,
-        mlp_t, activated, heads, query, key, value, heads_t, lse, cosine, sine,
-        merge_weight, query_weight, key_weight, value_weight, tokens, hidden, slope, cotangent, up_weight, down_weight,
-    )
-    wide = lambda a: a.transpose(1, 0, 2).reshape(width // chunks, -1)
-    tall = lambda a: a.transpose(0, 2, 1).reshape(-1, width // chunks)
-    grad_query, grad_key, grad_value = (wide(pieces[18 + k :: 3]) for k in range(3))
-    hits = (gathered[:, 16, :1] == jnp.arange(table_rows, dtype=jnp.float32)[None, :]).astype(jnp.float32)
-    mine = lax.axis_index("dp") * (width // chunks)
-    terms = gathered[:, :16].reshape(chunks, 2, width)
-    columns = lax.dynamic_slice_in_dim(terms, mine, width // chunks, axis=2).reshape(chunks, -1)
-    tables = jnp.dot(hits.T, columns, precision=highest)
-    grad_first, grad_second = jnp.split(tables, 2, axis=1)
-    return (
-        layer_output[None],
-        grad_tokens[None],
-        grad_query,
-        grad_key,
-        grad_value,
-        tall(pieces[16:18]),
-        wide(pieces[8:16]),
-        tall(pieces[:8]),
-        grad_first,
-        grad_second,
-    )
+        mlp_t, normal_mid, heads, query, key, value, heads_t, lse, cosine, sine,
+        merge_weight, query_weight, key_weight, value_weight, tokens, hidden, cotangent, up_weight, down_weight,
+    )
+    return finish(names, first_scales.shape[0], pieces, gathered, grad_tokens, layer_output)
 
 
 def body(

time: 288 us -> 256 us (0.89)
  Pallas kernels: 270 us -> 252 us
  local copies, waits for them, and re-layouts: 15.2 us -> 1.89 us
    pallas_call x1, Pallas kernels: 44.9 us -> 32.1 us  [forward(): pl.pallas_call(functools.partial(forward_kernel, names), out_shape=[jax.S...]
    pallas_call x1, Pallas kernels: 225 us -> 213 us  [backward(): pl.pallas_call(functools.partial(backward_kernel, names), out_shape=[jax....]
    pallas_call x0 -> x1, Pallas kernels: none -> 6.16 us  [finish(): pl.pallas_call(functools.partial(finish_kernel, names), out_shape=[jax.Sh...]
    unnamed x8 -> x0, local copies, waits for them, and re-layouts: 6.09 us -> none
    reshape x8 -> x0, local copies, waits for them, and re-layouts: 4.49 us -> none  [the longest x4 2.83 us: fast_body(): wide = lambda a: a.transpose(1, 0, 2).reshape(width // chunks, -1)]
where the time goes in v1:
time: 256 us
  Pallas kernels  252 us (98%)
    pallas_call x1, Pallas kernels, backward(): pl.pallas_call(functools.partial(backward_kernel, names), out_shape=[jax....  213 us
    pallas_call x1, Pallas kernels, forward(): pl.pallas_call(functools.partial(forward_kernel, names), out_shape=[jax.S...  32.1 us
    pallas_call x1, Pallas kernels, finish(): pl.pallas_call(functools.partial(finish_kernel, names), out_shape=[jax.Sh...  6.16 us

profile of v1, /device:TPU:0, one launch (start us, length us, event | category | flops | bytes accessed | tf_op | source)
XLA Modules:
  0.0 255.7 jit_solution(5320721403899634560)
XLA Ops:
  1.9 0.5 mul.3.moment
  2.5 1.4 constant_dynamic-slice_fusion
  3.8 32.1 %forward.1 = (bf16[4,1024,128]{2,1,0:T(8,128)(2,1)}, bf16[4,1024,128]{2,1,0:T(8,128)(2,1)}, bf16[4,1024,128]{2,1,0:T(8,128)(2,1)}, bf16[4,1024,128]{2,1,0:T(8,12...) custom-call(s32[1]{0:T(128)S(6)} %copy.24.length_ref, ...), custom_call_target="tpu_custom_call" | custom-call | tf_op jit(solution)/shard_map/forward/pallas_call | solution.py:287
  36.0 213.4 %backward.1 = (f32[24,64,256]{2,1,0:T(8,128)}, f32[16,24,128]{2,1,0:T(8,128)}, bf16[1024,1024]{1,0:T(8,128)(2,1)}, bf16[1024,1024]{1,0:T(8,128)(2,1)}, bf16[1024...) custom-call(s32[1]{0:T(128)S(6)} %copy.24.length_ref, ...), custom_call_target="tpu_custom_call" | custom-call | tf_op jit(solution)/shard_map/backward/pallas_call | solution.py:934
  249.4 6.2 %finish.1 = (bf16[1024,1024]{1,0:T(8,128)(2,1)}, bf16[1024,1024]{1,0:T(8,128)(2,1)}, f32[64,512]{1,0:T(8,128)}, f32[64,512]{1,0:T(8,128)}, f32[64,512]{1,0:T(8,1...) custom-call(f32[24,64,256]{2,1,0:T(8,128)} %get-tuple-element.42.pie, ...), custom_call_target="tpu_custom_call" | custom-call | tf_op jit(solution)/shard_map/finish/pallas_call | solution.py:1032

commit v2 on v1

--- a/solution.py
+++ b/solution.py
@@ -135,10 +135,10 @@
     loads = [
         pltpu.make_async_copy(a, b, wsem.at[i])
         for i, (a, b) in enumerate(
-            ((wq, vq), (wk, vk), (wv, vv), (cosine_in, cosine), (sine_in, sine), (wm, vm), (cotangent_in, cotangent))
+            ((wq, vq), (cosine_in, cosine), (sine_in, sine), (wk, vk), (wv, vv), (wm, vm), (cotangent_in, cotangent))
         )
     ]
-    for c in loads:
+    for c in loads[:5]:
         c.start()
     barrier = pltpu.get_barrier_semaphore()
     pl.semaphore_signal(barrier, inc=1, device_id=other, device_id_type=MESH)
@@ -160,14 +160,10 @@
         return 0
 
     lax.fori_loop(0, rows // 128, norm_rows, 0)
-    for c in loads:
+    for c in loads[5:]:
+        c.start()
+    for c in loads[:5]:
         c.wait()
-    send_m[...] = vm[...].astype(jnp.float32)
-    merge_copy = pltpu.make_async_remote_copy(
-        src_ref=send_m, dst_ref=recv_m, send_sem=ssem.at[0], recv_sem=rsem.at[0],
-        device_id=other, device_id_type=MESH,
-    )
-    merge_copy.start()
 
     def project(i, _):
         at = pl.multiple_of(i * 256, 256)
@@ -196,6 +192,15 @@
     ]
     for c in stores[:3]:
         c.start()
+    for c in loads[5:]:
+        c.wait()
+    send_m[...] = vm[...].astype(jnp.float32)
+    merge_copy = pltpu.make_async_remote_copy(
+        src_ref=send_m, dst_ref=recv_m, send_sem=ssem.at[0], recv_sem=rsem.at[0],
+        device_id=other, device_id_type=MESH,
+    )
+    merge_copy.start()
+
 
     def o_copy(p):
         return pltpu.make_async_remote_copy(
@@ -204,7 +209,7 @@
         )
 
     lane = lax.broadcasted_iota(jnp.int32, (rows, 128), 1)
-    block = 512
+    block = 1024
 
     def attend(p, _):
         for h in range(2):
@@ -341,9 +346,13 @@
     return 1 + (k * (k + 1)) // 2
 
 
+STARTS_Z = (2, 5, 10, 15, 19)
+
+
 def color_of(i):
-    turn = i - lax.div(i + 2, 5)
-    return jnp.where(lax.rem(i, 5) == 2, 2, lax.rem(turn, 2))
+    turn = i - count_from(i, [p + 1 for p in STARTS_Z])
+    on_z = sum(jnp.where(i == p, 1, 0) for p in STARTS_Z)
+    return jnp.where(on_z == 1, 2, lax.rem(turn, 2))
 
 
 def slot_of(i):
@@ -351,12 +360,12 @@
 
 
 def backward_kernel(
-    names, length_ref, moment, scale_one, scale_two,
+    names, length_ref, moment_ref, scale_one, scale_two,
     l_down, mid_in, heads, q_in, k_in, v_in, heads_t, lse_in, cosine, sine,
     merge_in, wq, wk, wv, tokens, hidden, cotangent, wu, wd,
     out, rows_out, tokens_out, layer_out, r_down, slope, r_up, hidden_grad,
     left, s1, r1, r2, r3, r4, rb, qkv, send_p, recv_p, ga, terms,
-    lsem, fsem, ssem, csem, psem, qsem, gsem, jsem, credit, credit_two, core_free,
+    msem, lsem, fsem, ssem, csem, psem, qsem, gsem, jsem, credit, credit_two, core_free,
 ):
     here = {n: lax.axis_index(n) for n in names}
     d = here[names[0]]
@@ -389,6 +398,8 @@
         for c in range(16):
             left[slot, absolute(c), :, own] = turned[64 * c : 64 * c + 64]
 
+    mid_load = pltpu.make_async_copy(mid_in, ga, msem)
+    mid_load.start()
     load_left(l_down, 0)
     barrier = pltpu.get_barrier_semaphore()
     for weight in (1, 2, 4, 8):
@@ -440,23 +451,28 @@
         )
 
     def tick(i):
-        a = i - LAGS[0]
-
-        @pl.when((a >= 0) & (a < ITEMS))
+        e = i - LAGS[3]
+
+        @pl.when((e >= 0) & (e < ITEMS))
         def _():
-            fetched(a, 1)
-            copy(a, 0).wait_recv()
-            r1[lax.rem(a, HELD)] += product(a, 0, 1)
-
-            @pl.when(a >= HELD)
-            def _():
-                pl.semaphore_wait(credit_two.at[color_of(a)], 1)
-
-            copy(a, 1).start()
-
-            @pl.when(a + 2 < ITEMS)
-            def _():
-                fetch(a + 2, 1)
+            copy(e, 3).wait_recv()
+            out[e] = r4[e, 0] + r3[e, 0]
+
+        c = i - LAGS[2]
+
+        @pl.when((c >= 0) & (c < ITEMS))
+        def _():
+            copy(c, 2).wait_recv()
+            r3[c] += r2[lax.rem(c, HELD), 0:2]
+            copy(c, 3).start()
+            copy(c, 2).wait_send()
+
+            @pl.when(c + HELD < ITEMS)
+            def _():
+                color = color_of(c + HELD)
+                pl.semaphore_signal(
+                    credit_two.at[color], inc=1, device_id=across(weight_of(color, 1)), device_id_type=MESH
+                )
 
         b = i - LAGS[1]
 
@@ -474,28 +490,23 @@
                     credit.at[color], inc=1, device_id=across(weight_of(color, 0)), device_id_type=MESH
                 )
 
-        c = i - LAGS[2]
-
-        @pl.when((c >= 0) & (c < ITEMS))
+        a = i - LAGS[0]
+
+        @pl.when((a >= 0) & (a < ITEMS))
         def _():
-            copy(c, 2).wait_recv()
-            r3[c] += r2[lax.rem(c, HELD), 0:2]
-            copy(c, 3).start()
-            copy(c, 2).wait_send()
-
-            @pl.when(c + HELD < ITEMS)
-            def _():
-                color = color_of(c + HELD)
-                pl.semaphore_signal(
-                    credit_two.at[color], inc=1, device_id=across(weight_of(color, 1)), device_id_type=MESH
-                )
-
-        e = i - LAGS[3]
-
-        @pl.when((e >= 0) & (e < ITEMS))
-        def _():
-            copy(e, 3).wait_recv()
-            out[e] = r4[e, 0] + r3[e, 0]
+            fetched(a, 1)
+            copy(a, 0).wait_recv()
+            r1[lax.rem(a, HELD)] += product(a, 0, 1)
+
+            @pl.when(a >= HELD)
+            def _():
+                pl.semaphore_wait(credit_two.at[color_of(a)], 1)
+
+            copy(a, 1).start()
+
+            @pl.when(a + 2 < ITEMS)
+            def _():
+                fetch(a + 2, 1)
 
         @pl.when(i < ITEMS)
         def _():
@@ -556,8 +567,6 @@
         lax.fori_loop(first, last, lambda i, _: (tick(i), 0)[1], 0)
 
     def mlp(vu, vd, cot, wide, hid, gp, gh, wsem, usem, dsem, tsem, osem):
-        mid_load = pltpu.make_async_copy(mid_in, ga, wsem.at[0])
-        mid_load.start()
         tiles = wu.shape[1] // TILE
 
         def columns(k):
@@ -566,10 +575,9 @@
         def up_load(k):
             return pltpu.make_async_copy(wu.at[:, columns(k)], vu.at[:, columns(k)], usem.at[k])
 
-        for k in range(tiles):
+        for k in range(2):
             up_load(k).start()
-        down_load = pltpu.make_async_copy(wd, vd, wsem.at[1])
-        down_load.start()
+        down_load = pltpu.make_async_copy(wd, vd, wsem)
 
         def tile_stores(k, lane):
             slot = lax.rem(k, 2)
@@ -587,6 +595,11 @@
                     x.wait()
 
             up_load(k).wait()
+
+            @pl.when(k + 2 < tiles)
+            def _():
+                up_load(k + 2).start()
+
             for r in range(0, rows, 512):
                 v = mm(ga[r : r + 512, :], vu[:, columns(k)])
                 square = v * v
@@ -627,6 +640,7 @@
             return 0
 
         lax.fori_loop(0, LAGS[0], early, 0)
+        down_load.start()
         lax.fori_loop(LAGS[0], tiles, lambda k, _: (up_tile(k, 1), 0)[1], 0)
         for k in (tiles - 2, tiles - 1):
             for x in tile_stores(k, 1):
@@ -737,7 +751,7 @@
         pltpu.VMEM((2, part, width), full),
         pltpu.VMEM((part, wu.shape[1]), half),
         pltpu.VMEM((part, width), full),
-        pltpu.SemaphoreType.DMA((2,)),
+        pltpu.SemaphoreType.DMA,
         pltpu.SemaphoreType.DMA((wu.shape[1] // TILE,)),
         pltpu.SemaphoreType.DMA((2, 2)),
         pltpu.SemaphoreType.DMA((3, 2)),
@@ -885,7 +899,7 @@
         core_sent(2)
         for j in range(8):
             terms[0, j : j + 1, :] = first[:, 128 * j : 128 * j + 128]
-        terms[0, 16:24, :] = jnp.broadcast_to(moment[...], (8, 128))
+        terms[0, 16:24, :] = jnp.full((8, 128), moment_ref[0].astype(full), full)
 
     pl.run_scoped(
         inner,
@@ -909,7 +923,17 @@
         exchange.start()
         tick(jnp.int32(done + stage))
         exchange.wait()
-    rows_out[...] = terms[...]
+    table_rows = rows_out.shape[1]
+    upper = lax.rem(d, 2) == 1
+    places = lax.broadcasted_iota(jnp.int32, (table_rows, 128), 0).astype(full)
+    total = jnp.zeros((table_rows, 128), full)
+    for n in range(16):
+        row = []
+        for base in (0, 8):
+            piece = terms[n, pl.ds(base + lax.div(d, 2), 1), :]
+            row.append(jnp.where(upper, piece[:, 64:], piece[:, :64]))
+        total = total + jnp.where(places == terms[n, 16:17, :], jnp.concatenate(row, axis=1), 0.0)
+    rows_out[...] = total.T
     run_ticks(done + 4, ITEMS + LAGS[3])
 
     def drain(i, _):
@@ -923,7 +947,7 @@
     lax.fori_loop(0, ITEMS, drain, 0)
 
 
-def backward(names, length, moment, scale_one, scale_two, *arrays):
+def backward(names, table_rows, length, moment, scale_one, scale_two, *arrays):
     tokens, up = arrays[-5], arrays[-2]
     rows, width = tokens.shape
     smem = pl.BlockSpec(memory_space=pltpu.SMEM)
@@ -935,7 +959,7 @@
         functools.partial(backward_kernel, names),
         out_shape=[
             jax.ShapeDtypeStruct((ITEMS, 64, TILE), full),
-            jax.ShapeDtypeStruct((16, 24, 128), full),
+            jax.ShapeDtypeStruct((128, table_rows), full),
             jax.ShapeDtypeStruct((rows, width), half),
             jax.ShapeDtypeStruct((rows, width), half),
             jax.ShapeDtypeStruct((rows, up.shape[1]), half),
@@ -943,7 +967,7 @@
             jax.ShapeDtypeStruct((rows, up.shape[1]), half),
             jax.ShapeDtypeStruct((rows, width), full),
         ],
-        in_specs=[smem] + [vmem] * 3 + [hbm] * len(arrays),
+        in_specs=[smem] * 2 + [vmem] * 2 + [hbm] * len(arrays),
         out_specs=[vmem] * 2 + [hbm] * 6,
         scratch_shapes=[
             pltpu.VMEM((3, 16, 64, rows), half),
@@ -958,6 +982,7 @@
             pltpu.VMEM((rows // 256, 256, width), full),
             pltpu.VMEM((rows, width), half),
             pltpu.VMEM((16, 24, 128), full),
+            dma,
             dma,
             dma((2, 2)),
             dma((4, ITEMS)),
@@ -978,69 +1003,61 @@
 
 
 def finish_kernel(
-    names, pieces, gathered, tokens_in, layer_in,
-    layer_out, tokens_out, grad_q, grad_k, grad_v, grad_m, grad_u, grad_d, first, second, held, sem,
+    pieces_in, tables_in, tokens_in, layer_in,
+    layer_out, tokens_out, grad_q, grad_k, grad_v, grad_m, grad_u, grad_d, first, second,
+    pieces, tables, held, isem, osem,
 ):
     parts = held.shape[1]
     step = layer_in.shape[0] // parts
-
-    def move(n, k):
-        source, target = ((layer_in, layer_out), (tokens_in, tokens_out))[n]
-        own = pl.ds(k * step, step)
-        return (
-            pltpu.make_async_copy(source.at[own, :], held.at[n, k], sem.at[0, n, k]),
-            pltpu.make_async_copy(held.at[n, k], target.at[own, :], sem.at[1, n, k]),
-        )
-
-    moves = [move(n, k) for n in range(2) for k in range(parts)]
-    for m in moves:
-        m[0].start()
-    for k in range(8):
-        grad_d[:, TILE * k : TILE * k + TILE] = pieces[k]
-        grad_u[:, TILE * k : TILE * k + TILE] = pieces[8 + k]
-    for k in range(2):
-        grad_m[:, TILE * k : TILE * k + TILE] = pieces[16 + k]
-        for n, ref in enumerate((grad_q, grad_k, grad_v)):
-            ref[:, TILE * k : TILE * k + TILE] = pieces[18 + 3 * k + n]
-    for m in moves:
-        m[0].wait()
-        m[1].start()
-    d = lax.axis_index(names[0])
-    count, table_rows = first.shape
-    upper = lax.rem(d, 2) == 1
-    places = lax.broadcasted_iota(jnp.int32, (table_rows, 128), 0).astype(jnp.float32)
-    total = jnp.zeros((table_rows, 128), jnp.float32)
-    for s in range(gathered.shape[0]):
-        row = []
-        for base in (0, 8):
-            part = gathered[s, pl.ds(base + lax.div(d, 2), 1), :]
-            row.append(jnp.where(upper, part[:, count:], part[:, :count]))
-        total = total + jnp.where(places == gathered[s, 16:17, :], jnp.concatenate(row, axis=1), 0.0)
-    turned = total.T
-    first[...] = turned[:count]
-    second[...] = turned[count:]
-    for m in moves:
-        m[1].wait()
-
-
-def finish(names, table_rows, pieces, gathered, tokens, layer):
-    vmem = pl.BlockSpec(memory_space=pltpu.VMEM)
+    incoming, outgoing = [], []
+
+    def move(source, keep, target):
+        n = len(incoming)
+        incoming.append(pltpu.make_async_copy(source, keep, isem.at[n]))
+        outgoing.append(pltpu.make_async_copy(keep, target, osem.at[n]))
+
+    for n, (source, target) in enumerate(((layer_in, layer_out), (tokens_in, tokens_out))):
+        for k in range(parts):
+            own = pl.ds(k * step, step)
+            move(source.at[own, :], held.at[n, k], target.at[own, :])
+    targets = [(grad_d, k) for k in range(8)] + [(grad_u, k) for k in range(8)] + [(grad_m, k) for k in range(2)]
+    targets += [(ref, k) for k in range(2) for ref in (grad_q, grad_k, grad_v)]
+    for n, (ref, k) in enumerate(targets):
+        move(pieces_in.at[n], pieces.at[n], ref.at[:, pl.ds(TILE * k, TILE)])
+    count = first.shape[0]
+    for k, ref in enumerate((first, second)):
+        own = pl.ds(k * count, count)
+        move(tables_in.at[own, :], tables.at[own, :], ref)
+    for c in incoming:
+        c.start()
+    for a, b in zip(incoming, outgoing):
+        a.wait()
+        b.start()
+    for c in outgoing:
+        c.wait()
+
+
+def finish(pieces, tables, tokens, layer):
     hbm = pl.BlockSpec(memory_space=pl.ANY)
     full = jnp.float32
     rows, width = layer.shape
+    table_rows = tables.shape[1]
     shapes = [(64, 512)] * 4 + [(64, 2048), (64, 2048), (64, table_rows), (64, table_rows)]
     layer, tokens, *grads = pl.pallas_call(
-        functools.partial(finish_kernel, names),
+        finish_kernel,
         out_shape=[jax.ShapeDtypeStruct(a.shape, a.dtype) for a in (layer, tokens)]
         + [jax.ShapeDtypeStruct(s, full) for s in shapes],
-        in_specs=[vmem] * 2 + [hbm] * 2,
-        out_specs=[hbm] * 2 + [vmem] * len(shapes),
+        in_specs=[hbm] * 4,
+        out_specs=[hbm] * (2 + len(shapes)),
         scratch_shapes=[
+            pltpu.VMEM(pieces.shape, full),
+            pltpu.VMEM(tables.shape, full),
             pltpu.VMEM((2, 4, rows // 4, width), layer.dtype),
-            pltpu.SemaphoreType.DMA((2, 2, 4)),
+            pltpu.SemaphoreType.DMA((34,)),
+            pltpu.SemaphoreType.DMA((34,)),
         ],
         name="finish",
-    )(pieces, gathered, tokens, layer)
+    )(pieces, tables, tokens, layer)
     query, key, value, merge, up, down, first, second = grads
     return layer[None], tokens[None], query, key, value, merge.T, up, down.T, first.T, second.T
 
@@ -1070,12 +1087,12 @@
         names, lengths, tokens, scale_one, scale_two, cotangent, cosine, sine,
         query_weight, key_weight, value_weight, merge_weight,
     )
-    pieces, gathered, grad_tokens, layer_output, *_ = backward(
-        names, lengths, jnp.full((1, 128), 1.0, jnp.float32) * moment.astype(jnp.float32), scale_one, scale_two,
+    pieces, tables, grad_tokens, layer_output, *_ = backward(
+        names, first_scales.shape[0], lengths, noise_times, scale_one, scale_two,
         mlp_t, normal_mid, heads, query, key, value, heads_t, lse, cosine, sine,
         merge_weight, query_weight, key_weight, value_weight, tokens, hidden, cotangent, up_weight, down_weight,
     )
-    return finish(names, first_scales.shape[0], pieces, gathered, grad_tokens, layer_output)
+    return finish(pieces, tables, grad_tokens, layer_output)
 
 
 def body(

time: 256 us -> 246 us (0.961)
  Pallas kernels: 252 us -> 242 us
    pallas_call x1, Pallas kernels: 213 us -> 208 us  [backward(): pl.pallas_call(functools.partial(backward_kernel, names), out_shape=[jax....]
    pallas_call x1, Pallas kernels: 32.1 us -> 28.9 us  [forward(): pl.pallas_call(functools.partial(forward_kernel, names), out_shape=[jax.S...]
where the time goes in v2:
time: 246 us
  Pallas kernels  242 us (98%)
    pallas_call x1, Pallas kernels, backward(): pl.pallas_call(functools.partial(backward_kernel, names), out_shape=[jax....  208 us
    pallas_call x1, Pallas kernels, forward(): pl.pallas_call(functools.partial(forward_kernel, names), out_shape=[jax.S...  28.9 us
    pallas_call x1, Pallas kernels, finish(): pl.pallas_call(finish_kernel, out_shape=[jax.ShapeDtypeStruct(a.shape, a....  5.56 us

profile of v2, /device:TPU:0, one launch (start us, length us, event | category | flops | bytes accessed | tf_op | source)
XLA Modules:
  0.0 245.7 jit_solution(2419004067960168601)
XLA Ops:
  1.9 1.4 constant_dynamic-slice_fusion
  3.3 28.9 %forward.1 = (bf16[4,1024,128]{2,1,0:T(8,128)(2,1)}, bf16[4,1024,128]{2,1,0:T(8,128)(2,1)}, bf16[4,1024,128]{2,1,0:T(8,128)(2,1)}, bf16[4,1024,128]{2,1,0:T(8,12...) custom-call(s32[1]{0:T(128)S(6)} %copy.24.length_ref, ...), custom_call_target="tpu_custom_call" | custom-call | tf_op jit(solution)/shard_map/forward/pallas_call | solution.py:292
  32.2 207.8 %backward.1 = (f32[24,64,256]{2,1,0:T(8,128)}, f32[128,256]{1,0:T(8,128)}, bf16[1024,1024]{1,0:T(8,128)(2,1)}, bf16[1024,1024]{1,0:T(8,128)(2,1)}, bf16[1024,204...) custom-call(s32[1]{0:T(128)S(6)} %copy.24.length_ref, ...), custom_call_target="tpu_custom_call" | custom-call | tf_op jit(solution)/shard_map/backward/pallas_call | solution.py:958
  240.0 5.6 %finish.1 = (bf16[1024,1024]{1,0:T(8,128)(2,1)}, bf16[1024,1024]{1,0:T(8,128)(2,1)}, f32[64,512]{1,0:T(8,128)}, f32[64,512]{1,0:T(8,128)}, f32[64,512]{1,0:T(8,1...) custom-call(f32[24,64,256]{2,1,0:T(8,128)} %get-tuple-element.42.pie, ...), custom_call_target="tpu_custom_call" | custom-call | tf_op jit(solution)/shard_map/finish/pallas_call | solution.py:1046

commit v3 on v2

--- a/solution.py
+++ b/solution.py
@@ -122,10 +122,10 @@
 
 
 def forward_kernel(
-    names, length_ref, tokens, scale_one, scale_two, cotangent_in, cosine_in, sine_in, wq, wk, wv, wm,
-    q_hbm, k_hbm, v_hbm, heads_hbm, heads_t_hbm, lse_hbm, hidden_hbm, mid_hbm, mlp_t_hbm,
-    q_out, k_out, v_out, heads, heads_t, lse, hidden, mid, mlp_t, cotangent, cosine, sine,
-    nin, vq, vk, vv, vm, other_m, v_t, send_m, recv_m, send_o, recv_o, bias, wsem, osem, tsem, ssem, rsem,
+    names, length_ref, moment_ref, tokens, first_in, second_in, cotangent_in, cosine_in, sine_in, wq, wk, wv, wm,
+    q_hbm, k_hbm, v_hbm, heads_hbm, heads_t_hbm, lse_hbm, hidden_hbm, mid_hbm, mlp_t_hbm, one_hbm, two_hbm,
+    q_out, k_out, v_out, heads, heads_t, lse, hidden, mid, mlp_t, scale_one, scale_two, cotangent, cosine, sine,
+    first_scales, second_scales, nin, vq, vk, vv, vm, other_m, v_t, send_m, recv_m, send_o, recv_o, bias, wsem, osem, tsem, ssem, rsem,
 ):
     rows, width = tokens.shape
     pairs = q_out.shape[0]
@@ -135,10 +135,11 @@
     loads = [
         pltpu.make_async_copy(a, b, wsem.at[i])
         for i, (a, b) in enumerate(
-            ((wq, vq), (cosine_in, cosine), (sine_in, sine), (wk, vk), (wv, vv), (wm, vm), (cotangent_in, cotangent))
+            ((first_in, first_scales), (wq, vq), (cosine_in, cosine), (sine_in, sine), (wk, vk), (wv, vv), (wm, vm),
+             (cotangent_in, cotangent), (second_in, second_scales))
         )
     ]
-    for c in loads[:5]:
+    for c in loads[:6]:
         c.start()
     barrier = pltpu.get_barrier_semaphore()
     pl.semaphore_signal(barrier, inc=1, device_id=other, device_id_type=MESH)
@@ -153,6 +154,9 @@
 
     bias[...] = jnp.broadcast_to((mask_of(0, rows) - 1.0) * 1000000000.0, (rows, 128))
 
+    loads[0].wait()
+    scale_one[...] = first_scales[pl.ds(moment_ref[0], 1), :]
+
     def norm_rows(i, _):
         at = pl.multiple_of(i * 128, 128)
         x = tokens[pl.ds(at, 128), :].astype(jnp.float32) * mask_of(at, 128)
@@ -160,9 +164,9 @@
         return 0
 
     lax.fori_loop(0, rows // 128, norm_rows, 0)
-    for c in loads[5:]:
+    for c in loads[6:]:
         c.start()
-    for c in loads[:5]:
+    for c in loads[1:6]:
         c.wait()
 
     def project(i, _):
@@ -187,13 +191,14 @@
         pltpu.make_async_copy(a, b, osem.at[i])
         for i, (a, b) in enumerate(
             ((q_out, q_hbm), (k_out, k_hbm), (v_out, v_hbm), (heads, heads_hbm), (heads_t, heads_t_hbm), (lse, lse_hbm),
-             (mlp_t, mlp_t_hbm))
+             (mlp_t, mlp_t_hbm), (scale_one, one_hbm), (scale_two, two_hbm))
         )
     ]
     for c in stores[:3]:
         c.start()
-    for c in loads[5:]:
+    for c in loads[6:]:
         c.wait()
+    scale_two[...] = second_scales[pl.ds(moment_ref[0], 1), :]
     send_m[...] = vm[...].astype(jnp.float32)
     merge_copy = pltpu.make_async_remote_copy(
         src_ref=send_m, dst_ref=recv_m, send_sem=ssem.at[0], recv_sem=rsem.at[0],
@@ -237,6 +242,13 @@
     lax.fori_loop(0, pairs, attend, 0)
     for c in stores[3:]:
         c.start()
+
+    def merge_own(i, _):
+        own = pl.ds(pl.multiple_of(i * 256, 256), 256)
+        hidden[own, :] = mm(jnp.concatenate([heads[p, own, :] for p in range(pairs)], axis=1), vm[...])
+        return 0
+
+    lax.fori_loop(0, rows // 256, merge_own, 0)
     merge_copy.wait()
     other_m[...] = recv_m[...].astype(jnp.bfloat16)
     for p in range(pairs):
@@ -252,9 +264,8 @@
     def finish(i, _):
         at = pl.multiple_of(i * 256, 256)
         own = pl.ds(at, 256)
-        mine = jnp.concatenate([heads[p, own, :] for p in range(pairs)], axis=1)
         theirs = jnp.concatenate([recv_o[p, own, :].astype(jnp.bfloat16) for p in range(pairs)], axis=1)
-        attn = mm(mine, vm[...]) + mm(theirs, other_m[...])
+        attn = hidden[own, :] + mm(theirs, other_m[...])
         one = tokens[own, :].astype(jnp.float32) * mask_of(at, 256) + attn
         hidden[own, :] = one
         mid[own, :] = (centre(one) * scale_two[...]).astype(jnp.bfloat16)
@@ -270,7 +281,7 @@
             c.wait()
 
 
-def forward(names, length, tokens, scale_one, scale_two, cotangent, cosine, sine, wq, wk, wv, wm):
+def forward(names, length, moment, tokens, first_scales, second_scales, cotangent, cosine, sine, wq, wk, wv, wm):
     rows, width = tokens.shape
     local = wq.shape[1]
     pairs = local // 128
@@ -288,17 +299,21 @@
         ((rows, width), full),
         ((rows, width), half),
         ((16, width // 16, rows), half),
+        ((1, width), full),
+        ((1, width), full),
     ]
     return pl.pallas_call(
         functools.partial(forward_kernel, names),
         out_shape=[jax.ShapeDtypeStruct(*s) for s in shapes],
-        in_specs=[pl.BlockSpec(memory_space=pltpu.SMEM)] + [vmem] * 3 + [hbm] * 7,
+        in_specs=[pl.BlockSpec(memory_space=pltpu.SMEM)] * 2 + [vmem] + [hbm] * 9,
         out_specs=[hbm] * len(shapes),
         scratch_shapes=[pltpu.VMEM(*s) for s in shapes]
         + [
             pltpu.VMEM((rows, width), half),
             pltpu.VMEM((rows, 128), full),
             pltpu.VMEM((rows, 128), full),
+            pltpu.VMEM(first_scales.shape, full),
+            pltpu.VMEM(second_scales.shape, full),
             pltpu.VMEM((rows, width), half),
             pltpu.VMEM(wq.shape, half),
             pltpu.VMEM(wk.shape, half),
@@ -311,15 +326,15 @@
             pltpu.VMEM((pairs, rows, 128), full),
             pltpu.VMEM((pairs, rows, 128), full),
             pltpu.VMEM((rows, 128), full),
-            pltpu.SemaphoreType.DMA((7,)),
-            pltpu.SemaphoreType.DMA((7,)),
+            pltpu.SemaphoreType.DMA((9,)),
+            pltpu.SemaphoreType.DMA((9,)),
             pltpu.SemaphoreType.DMA((2, 4)),
             pltpu.SemaphoreType.DMA((1 + pairs,)),
             pltpu.SemaphoreType.DMA((1 + pairs,)),
         ],
         compiler_params=pltpu.CompilerParams(collective_id=1, has_side_effects=True, vmem_limit_bytes=58 * 2**20),
         name="forward",
-    )(length, tokens, scale_one, scale_two, cotangent, cosine, sine, wq, wk, wv, wm)
+    )(length, moment, tokens, first_scales, second_scales, cotangent, cosine, sine, wq, wk, wv, wm)
 
 
 ITEMS = 24
@@ -365,7 +380,7 @@
     merge_in, wq, wk, wv, tokens, hidden, cotangent, wu, wd,
     out, rows_out, tokens_out, layer_out, r_down, slope, r_up, hidden_grad,
     left, s1, r1, r2, r3, r4, rb, qkv, send_p, recv_p, ga, terms,
-    msem, lsem, fsem, ssem, csem, psem, qsem, gsem, jsem, credit, credit_two, core_free,
+    msem, lsem, rsem, fsem, ssem, csem, psem, qsem, gsem, jsem, credit, credit_two, core_free,
 ):
     here = {n: lax.axis_index(n) for n in names}
     d = here[names[0]]
@@ -450,13 +465,17 @@
             device_id=across(weight), device_id_type=MESH,
         )
 
+    def result(i):
+        return pltpu.make_async_copy(r4.at[i, 0], out.at[i], rsem.at[i])
+
     def tick(i):
         e = i - LAGS[3]
 
         @pl.when((e >= 0) & (e < ITEMS))
         def _():
             copy(e, 3).wait_recv()
-            out[e] = r4[e, 0] + r3[e, 0]
+            r4[e, 0] = r4[e, 0] + r3[e, 0]
+            result(e).start()
 
         c = i - LAGS[2]
 
@@ -942,6 +961,7 @@
             copy(i, 0).wait_send()
 
         copy(i, 3).wait_send()
+        result(i).wait()
         return 0
 
     lax.fori_loop(0, ITEMS, drain, 0)
@@ -968,7 +988,7 @@
             jax.ShapeDtypeStruct((rows, width), full),
         ],
         in_specs=[smem] * 2 + [vmem] * 2 + [hbm] * len(arrays),
-        out_specs=[vmem] * 2 + [hbm] * 6,
+        out_specs=[hbm, vmem] + [hbm] * 6,
         scratch_shapes=[
             pltpu.VMEM((3, 16, 64, rows), half),
             pltpu.VMEM((RING, 8, 64, TILE), full),
@@ -984,6 +1004,7 @@
             pltpu.VMEM((16, 24, 128), full),
             dma,
             dma,
+            dma((ITEMS,)),
             dma((2, 2)),
             dma((4, ITEMS)),
             dma((4, ITEMS)),
@@ -1052,9 +1073,9 @@
         scratch_shapes=[
             pltpu.VMEM(pieces.shape, full),
             pltpu.VMEM(tables.shape, full),
-            pltpu.VMEM((2, 4, rows // 4, width), layer.dtype),
-            pltpu.SemaphoreType.DMA((34,)),
-            pltpu.SemaphoreType.DMA((34,)),
+            pltpu.VMEM((2, 1, rows // 1, width), layer.dtype),
+            pltpu.SemaphoreType.DMA((28,)),
+            pltpu.SemaphoreType.DMA((28,)),
         ],
         name="finish",
     )(pieces, tables, tokens, layer)
@@ -1079,12 +1100,9 @@
     tokens, cotangent = tokens[0], cotangent[0]
     rows, width = tokens.shape
     names = ("dp", "tensor")
-    moment = noise_times[0]
-    scale_one = lax.dynamic_slice_in_dim(first_scales, moment, 1, axis=0)
-    scale_two = lax.dynamic_slice_in_dim(second_scales, moment, 1, axis=0)
     cosine, sine = (jnp.asarray(a) for a in rope_lanes(rows))
-    query, key, value, heads, heads_t, lse, hidden, normal_mid, mlp_t = forward(
-        names, lengths, tokens, scale_one, scale_two, cotangent, cosine, sine,
+    query, key, value, heads, heads_t, lse, hidden, normal_mid, mlp_t, scale_one, scale_two = forward(
+        names, lengths, noise_times, tokens, first_scales, second_scales, cotangent, cosine, sine,
         query_weight, key_weight, value_weight, merge_weight,
     )
     pieces, tables, grad_tokens, layer_output, *_ = backward(

time: 246 us -> 244 us (level)
  no operation moved by 1% of the time
where the time goes in v3:
time: 244 us
  Pallas kernels  242 us (99%)
    pallas_call x1, Pallas kernels, backward(): pl.pallas_call(functools.partial(backward_kernel, names), out_shape=[jax....  208 us
    pallas_call x1, Pallas kernels, forward(): pl.pallas_call(functools.partial(forward_kernel, names), out_shape=[jax.S...  29.2 us

profile of v3, /device:TPU:0, one launch (start us, length us, event | category | flops | bytes accessed | tf_op | source)
XLA Modules:
  0.0 243.7 jit_solution(16862174640253699589)
XLA Ops:
  1.9 29.2 %forward.1 = (bf16[4,1024,128]{2,1,0:T(8,128)(2,1)}, bf16[4,1024,128]{2,1,0:T(8,128)(2,1)}, bf16[4,1024,128]{2,1,0:T(8,128)(2,1)}, bf16[4,1024,128]{2,1,0:T(8,12...) custom-call(s32[1]{0:T(128)S(6)} %copy.24.length_ref, ...), custom_call_target="tpu_custom_call" | custom-call | tf_op jit(solution)/shard_map/forward/pallas_call | solution.py:305
  31.2 207.8 %backward.1 = (f32[24,64,256]{2,1,0:T(8,128)}, f32[128,256]{1,0:T(8,128)}, bf16[1024,1024]{1,0:T(8,128)(2,1)}, bf16[1024,1024]{1,0:T(8,128)(2,1)}, bf16[1024,204...) custom-call(s32[1]{0:T(128)S(6)} %copy.24.length_ref, ...), custom_call_target="tpu_custom_call" | custom-call | tf_op jit(solution)/shard_map/backward/pallas_call | solution.py:978
  238.9 4.6 %finish.1 = (bf16[1024,1024]{1,0:T(8,128)(2,1)}, bf16[1024,1024]{1,0:T(8,128)(2,1)}, f32[64,512]{1,0:T(8,128)}, f32[64,512]{1,0:T(8,128)}, f32[64,512]{1,0:T(8,1...) custom-call(f32[24,64,256]{2,1,0:T(8,128)} %get-tuple-element.46.pie, ...), custom_call_target="tpu_custom_call" | custom-call | tf_op jit(solution)/shard_map/finish/pallas_call | solution.py:1067

commit v4 on v3

--- a/solution.py
+++ b/solution.py
@@ -1043,18 +1043,26 @@
             move(source.at[own, :], held.at[n, k], target.at[own, :])
     targets = [(grad_d, k) for k in range(8)] + [(grad_u, k) for k in range(8)] + [(grad_m, k) for k in range(2)]
     targets += [(ref, k) for k in range(2) for ref in (grad_q, grad_k, grad_v)]
-    for n, (ref, k) in enumerate(targets):
-        move(pieces_in.at[n], pieces.at[n], ref.at[:, pl.ds(TILE * k, TILE)])
     count = first.shape[0]
     for k, ref in enumerate((first, second)):
         own = pl.ds(k * count, count)
         move(tables_in.at[own, :], tables.at[own, :], ref)
+    results = []
+    for n, (ref, k) in enumerate(targets):
+        results.append(
+            pltpu.make_async_copy(pieces.at[n], ref.at[:, pl.ds(TILE * k, TILE)], osem.at[len(incoming) + n])
+        )
+    whole = pltpu.make_async_copy(pieces_in, pieces, isem.at[len(incoming)])
+    whole.start()
     for c in incoming:
+        c.start()
+    whole.wait()
+    for c in results:
         c.start()
     for a, b in zip(incoming, outgoing):
         a.wait()
         b.start()
-    for c in outgoing:
+    for c in results + outgoing:
         c.wait()
 
 

time: 244 us -> 245 us (level)
  no operation moved by 1% of the time
where the time goes in v4:
time: 245 us; the launch traced here: 244 us
  Pallas kernels  242 us (99%)
    pallas_call x1, Pallas kernels, backward(): pl.pallas_call(functools.partial(backward_kernel, names), out_shape=[jax....  208 us
    pallas_call x1, Pallas kernels, forward(): pl.pallas_call(functools.partial(forward_kernel, names), out_shape=[jax.S...  29.2 us
    pallas_call x1, Pallas kernels, finish(): pl.pallas_call(finish_kernel, out_shape=[jax.ShapeDtypeStruct(a.shape, a....  5.28 us

profile of v4, /device:TPU:0, one launch (start us, length us, event | category | flops | bytes accessed | tf_op | source)
XLA Modules:
  0.0 244.4 jit_solution(12110412702775834698)
XLA Ops:
  1.9 29.2 %forward.1 = (bf16[4,1024,128]{2,1,0:T(8,128)(2,1)}, bf16[4,1024,128]{2,1,0:T(8,128)(2,1)}, bf16[4,1024,128]{2,1,0:T(8,128)(2,1)}, bf16[4,1024,128]{2,1,0:T(8,12...) custom-call(s32[1]{0:T(128)S(6)} %copy.24.length_ref, ...), custom_call_target="tpu_custom_call" | custom-call | tf_op jit(solution)/shard_map/forward/pallas_call | solution.py:305
  31.2 207.8 %backward.1 = (f32[24,64,256]{2,1,0:T(8,128)}, f32[128,256]{1,0:T(8,128)}, bf16[1024,1024]{1,0:T(8,128)(2,1)}, bf16[1024,1024]{1,0:T(8,128)(2,1)}, bf16[1024,204...) custom-call(s32[1]{0:T(128)S(6)} %copy.24.length_ref, ...), custom_call_target="tpu_custom_call" | custom-call | tf_op jit(solution)/shard_map/backward/pallas_call | solution.py:978
  238.9 5.3 %finish.1 = (bf16[1024,1024]{1,0:T(8,128)(2,1)}, bf16[1024,1024]{1,0:T(8,128)(2,1)}, f32[64,512]{1,0:T(8,128)}, f32[64,512]{1,0:T(8,128)}, f32[64,512]{1,0:T(8,1...) custom-call(f32[24,64,256]{2,1,0:T(8,128)} %get-tuple-element.46.pie, ...), custom_call_target="tpu_custom_call" | custom-call | tf_op jit(solution)/shard_map/finish/pallas_call | solution.py:1075
